TPU v7x, 32 devices: a whole 2x2x4 slice. The times are simulated.
32 devices in a mesh: dp: 8 (over z, x), tensor: 4 (over y, core).
Axes of the slice: x: 2, y: 2, z: 4, core: 2. Of those that a mesh axis runs over, the one named last changes fastest.
Arguments:
- tokens: bfloat16 [16384, 768], P(('dp', 'tensor')), may hold values from -6 to 6
- segment_ids: int32 [16, 1024], P('dp'), may hold values from 0 to 3, never falling along the last dimension, each value on 1 to 512 neighbouring positions
- ln1_gain: float32 [768], replicated, may hold values from 0.5 to 1.5
- ln1_bias: float32 [768], replicated, may hold values from -3 to 3
- w_qkv: bfloat16 [768, 3, 768], P(None, None, 'tensor'), may hold values from -0.21875 to 0.21875
- b_qv: float32 [2, 768], P(None, 'tensor'), may hold values from -3 to 3
- w_out: bfloat16 [768, 768], P('tensor'), may hold values from -0.875 to 0.875
- b_out: float32 [768], replicated, may hold values from -3 to 3
- ln2_gain: float32 [768], replicated, may hold values from 0.5 to 1.5
- ln2_bias: float32 [768], replicated, may hold values from -3 to 3
- w_fc: bfloat16 [768, 3072], P(None, 'tensor'), may hold values from -0.21875 to 0.21875
- b_fc: float32 [3072], P('tensor'), may hold values from -3 to 3
- w_proj: bfloat16 [3072, 768], P('tensor'), may hold values from -0.109375 to 0.109375
- b_proj: float32 [768], replicated, may hold values from -3 to 3
- cotangent: bfloat16 [16384, 768], P(('dp', 'tensor')), may hold values from -6 to 6
Outputs:
- output: bfloat16 [16384, 768], P(('dp', 'tensor'))
- d_tokens: float32 [16384, 768], P(('dp', 'tensor'))
- d_ln1_gain: float32 [768], replicated
- d_ln1_bias: float32 [768], replicated
- d_w_qkv: float32 [768, 3, 768], P(None, None, 'tensor')
- d_b_qv: float32 [2, 768], P(None, 'tensor')
- d_w_out: float32 [768, 768], P('tensor')
- d_b_out: float32 [768], replicated
- d_ln2_gain: float32 [768], replicated
- d_ln2_bias: float32 [768], replicated
- d_w_fc: float32 [768, 3072], P(None, 'tensor')
- d_b_fc: float32 [3072], P('tensor')
- d_w_proj: float32 [3072, 768], P('tensor')
- d_b_proj: float32 [768], replicated
Inputs may be any that keep to these rules, and one draw needn't show every extreme that they name: `segment_ids`: within each packed sequence the document numbers never fall; every document holds 1 to 512 tokens, one exactly 512.
All inputs are finite; a program needn't handle non-finite values.
Results may differ from a plain program's by a relative error of at most 0.012.
Values may be sent and summed in bfloat16 or wider, within the bound.
A program may use at most 128 MiB of HBM per device.

v0:
```python
import jax
import jax.numpy as jnp
from jax import lax
from jax.sharding import PartitionSpec as P

HD = 64


NEG_FILL = -1e30


def layer_norm(values, norm_gain, norm_shift):
    center = values - jnp.mean(values, -1, keepdims=True)
    variance = jnp.mean(center * center, -1, keepdims=True)
    return center * lax.rsqrt(variance + 1e-05) * norm_gain + norm_shift


def allowed_mask(segment, offset, block_size):
    positions = jnp.arange(segment.shape[0])
    query_pos = positions[offset : offset + block_size]
    query_seg = segment[offset : offset + block_size]
    return (positions[None, :] <= query_pos[:, None]) & (segment[None, :] == query_seg[:, None])


def attend(inputs):
    queries, key_rows, value_rows, segment = inputs
    seq_len = segment.shape[0]
    block_size = min(512, seq_len)
    scale = key_rows.shape[-1] ** (-0.5)
    outputs = []
    log_parts = []
    for offset in range(0, seq_len, block_size):
        query_block = queries[offset : offset + block_size]
        allowed = allowed_mask(segment, offset, block_size)
        scores = (
            jnp.einsum("qhe,khe->hqk", query_block, key_rows, preferred_element_type=jnp.float32)
            * scale
        )
        scores = jnp.where(allowed[None], scores, NEG_FILL)
        top_score = jnp.max(scores, -1, keepdims=True)
        expo_vals = jnp.exp(scores - top_score)
        row_total = jnp.sum(expo_vals, -1, keepdims=True)
        attn_probs = (expo_vals / row_total).astype(jnp.bfloat16)
        outputs.append(
            jnp.einsum("hqk,khe->qhe", attn_probs, value_rows, preferred_element_type=jnp.float32)
        )
        log_parts.append((top_score + jnp.log(row_total))[..., 0])
    return (jnp.concatenate(outputs, 0), jnp.concatenate(log_parts, 1))


def attend_back(inputs):
    queries, key_rows, value_rows, grad_out, log_sums, segment = inputs
    seq_len = segment.shape[0]
    block_size = min(512, seq_len)
    scale = key_rows.shape[-1] ** (-0.5)
    grad_keys = jnp.zeros(key_rows.shape, jnp.float32)
    grad_values = jnp.zeros(value_rows.shape, jnp.float32)
    query_parts = []
    for offset in range(0, seq_len, block_size):
        query_block = queries[offset : offset + block_size]
        grad_block = grad_out[offset : offset + block_size]
        allowed = allowed_mask(segment, offset, block_size)
        scores = (
            jnp.einsum("qhe,khe->hqk", query_block, key_rows, preferred_element_type=jnp.float32)
            * scale
        )
        block_logs = log_sums[:, offset : offset + block_size, None]
        attn_probs = jnp.where(allowed[None], jnp.exp(scores - block_logs), 0.0)
        grad_probs = jnp.einsum(
            "qhe,khe->hqk", grad_block, value_rows, preferred_element_type=jnp.float32
        )
        inner_sum = jnp.sum(attn_probs * grad_probs, -1, keepdims=True)
        grad_scores = (attn_probs * (grad_probs - inner_sum)).astype(jnp.bfloat16)
        query_parts.append(
            jnp.einsum("hqk,khe->qhe", grad_scores, key_rows, preferred_element_type=jnp.float32)
            * scale
        )
        grad_keys = (
            grad_keys
            + jnp.einsum(
                "hqk,qhe->khe", grad_scores, query_block, preferred_element_type=jnp.float32
            )
            * scale
        )
        grad_values = grad_values + jnp.einsum(
            "hqk,qhe->khe",
            attn_probs.astype(jnp.bfloat16),
            grad_block,
            preferred_element_type=jnp.float32,
        )
    return (jnp.concatenate(query_parts, 0), grad_keys, grad_values)


def on_device(
    tokens,
    segment_ids,
    ln1_gain,
    ln1_bias,
    w_qkv,
    b_qv,
    w_out,
    b_out,
    ln2_gain,
    ln2_bias,
    w_fc,
    b_fc,
    w_proj,
    b_proj,
    cotangent,
):
    row_count = tokens.shape[0]
    model_width = tokens.shape[1]
    pack_count = segment_ids.shape[0]
    seq_len = segment_ids.shape[1]
    local_width = w_qkv.shape[2]
    hidden_width = w_fc.shape[1]
    local_heads = local_width // HD
    total_rows = pack_count * seq_len
    head_shape = (pack_count, seq_len, local_heads, HD)
    x_full = tokens.astype(jnp.float32)
    normed = layer_norm(x_full, ln1_gain, ln1_bias).astype(jnp.bfloat16)
    normed_all = lax.all_gather(normed, "tensor", axis=0, tiled=True)
    packed = jnp.einsum("td,dcn->tcn", normed_all, w_qkv, preferred_element_type=jnp.float32)
    queries = (packed[:, 0] + b_qv[0]).astype(jnp.bfloat16).reshape(head_shape)
    key_rows = packed[:, 1].astype(jnp.bfloat16).reshape(head_shape)
    value_rows = (packed[:, 2] + b_qv[1]).astype(jnp.bfloat16).reshape(head_shape)
    attn_heads, log_sums = lax.map(attend, (queries, key_rows, value_rows, segment_ids))
    mixed_heads = attn_heads.reshape(total_rows, local_width).astype(jnp.bfloat16)
    residual = (
        x_full
        + lax.psum_scatter(
            jnp.dot(
                lax.slice_in_dim(mixed_heads, 0, row_count * lax.axis_size("tensor"), axis=0),
                w_out,
                preferred_element_type=jnp.float32,
            ),
            "tensor",
            scatter_dimension=0,
            tiled=True,
        )
        + b_out
    )
    normed2 = layer_norm(residual, ln2_gain, ln2_bias).astype(jnp.bfloat16)
    normed2_all = lax.all_gather(normed2, "tensor", axis=0, tiled=True)
    pre_act = jnp.dot(normed2_all, w_fc, preferred_element_type=jnp.float32) + b_fc
    hidden = jax.nn.gelu(pre_act, approximate=True).astype(jnp.bfloat16)
    output = (
        residual
        + lax.psum_scatter(
            jnp.dot(
                lax.slice_in_dim(hidden, 0, row_count * lax.axis_size("tensor"), axis=0),
                w_proj,
                preferred_element_type=jnp.float32,
            ).astype(jnp.bfloat16),
            "tensor",
            scatter_dimension=0,
            tiled=True,
        ).astype(jnp.float32)
        + b_proj
    ).astype(jnp.bfloat16)
    cot_full = cotangent.astype(jnp.float32)
    shard_rows = lax.all_gather(cotangent, "tensor", axis=0, tiled=True)
    grad_proj = jnp.zeros((hidden_width, model_width), jnp.float32)
    row_span = shard_rows.shape[0]
    rows_grad = jnp.dot(shard_rows, w_proj.T, preferred_element_type=jnp.float32)
    grad_buffer = rows_grad
    hidden_part = lax.slice_in_dim(hidden, 0, row_span, axis=0)
    grad_hidden = grad_buffer
    d_w_proj = grad_proj + jnp.dot(hidden_part.T, shard_rows, preferred_element_type=jnp.float32)
    gelu_value, gelu_back = jax.vjp(lambda inner: jax.nn.gelu(inner, approximate=True), pre_act)
    grad_pre = gelu_back(grad_hidden)[0].astype(jnp.bfloat16)
    d_b_fc = jnp.sum(grad_pre.astype(jnp.float32), 0)
    d_w_fc = jnp.dot(normed2_all.T, grad_pre, preferred_element_type=jnp.float32)
    grad_normed2 = lax.psum_scatter(
        jnp.dot(
            lax.slice_in_dim(grad_pre, 0, row_count * lax.axis_size("tensor"), axis=0),
            w_fc.T,
            preferred_element_type=jnp.float32,
        ),
        "tensor",
        scatter_dimension=0,
        tiled=True,
    )
    norm_value, ln2_back = jax.vjp(layer_norm, residual, ln2_gain, ln2_bias)
    grad_resid_part, d_ln2_gain, d_ln2_bias = ln2_back(grad_normed2)
    grad_resid = cot_full + grad_resid_part
    d_b_proj = jnp.sum(cot_full, 0)
    d_b_out = jnp.sum(grad_resid, 0)
    resid_low = grad_resid.astype(jnp.bfloat16)
    shard_rows = lax.all_gather(resid_low, "tensor", axis=0, tiled=True)
    row_start = jnp.int32(0)
    grad_buffer = jnp.zeros((total_rows, local_width), jnp.float32)
    grad_outw = jnp.zeros((local_width, model_width), jnp.float32)
    row_span = shard_rows.shape[0]
    rows_grad = jnp.dot(shard_rows, w_out.T, preferred_element_type=jnp.float32)
    grad_buffer = lax.dynamic_update_slice_in_dim(grad_buffer, rows_grad, row_start, 0)
    mixed_part = lax.dynamic_slice_in_dim(mixed_heads, row_start, row_span, 0)
    d_w_out = grad_outw + jnp.dot(mixed_part.T, shard_rows, preferred_element_type=jnp.float32)
    grad_mixed_low = grad_buffer.astype(jnp.bfloat16).reshape(head_shape)
    grad_query, grad_key, grad_value = lax.map(
        attend_back, (queries, key_rows, value_rows, grad_mixed_low, log_sums, segment_ids)
    )
    grad_query = grad_query.reshape(total_rows, local_width).astype(jnp.bfloat16)
    grad_key = grad_key.reshape(total_rows, local_width).astype(jnp.bfloat16)
    grad_value = grad_value.reshape(total_rows, local_width).astype(jnp.bfloat16)
    d_b_qv = jnp.stack(
        [jnp.sum(grad_query.astype(jnp.float32), 0), jnp.sum(grad_value.astype(jnp.float32), 0)]
    )
    grad_packed = jnp.stack([grad_query, grad_key, grad_value], axis=1)
    d_w_qkv = jnp.einsum("td,tcn->dcn", normed_all, grad_packed, preferred_element_type=jnp.float32)
    rows_part = lax.slice_in_dim(grad_packed, 0, row_count * lax.axis_size("tensor"), axis=0)
    grad_normed = lax.psum_scatter(
        jnp.einsum("tcn,dcn->td", rows_part, w_qkv, preferred_element_type=jnp.float32),
        "tensor",
        scatter_dimension=0,
        tiled=True,
    )
    first_value, ln1_back = jax.vjp(layer_norm, x_full, ln1_gain, ln1_bias)
    grad_tok_part, d_ln1_gain, d_ln1_bias = ln1_back(grad_normed)
    d_tokens = grad_resid + grad_tok_part
    d_w_qkv, d_b_qv, d_w_out, d_w_fc, d_b_fc, d_w_proj = lax.psum(
        (d_w_qkv, d_b_qv, d_w_out, d_w_fc, d_b_fc, d_w_proj), "dp"
    )
    d_ln1_gain, d_ln1_bias, d_b_out, d_ln2_gain, d_ln2_bias, d_b_proj = lax.psum(
        (d_ln1_gain, d_ln1_bias, d_b_out, d_ln2_gain, d_ln2_bias, d_b_proj), ("dp", "tensor")
    )
    return (
        output,
        d_tokens,
        d_ln1_gain,
        d_ln1_bias,
        d_w_qkv,
        d_b_qv,
        d_w_out,
        d_b_out,
        d_ln2_gain,
        d_ln2_bias,
        d_w_fc,
        d_b_fc,
        d_w_proj,
        d_b_proj,
    )


def solution(mesh):
    return jax.shard_map(
        on_device,
        mesh=mesh,
        in_specs=(
            P(("dp", "tensor"), None),
            P("dp", None),
            P(),
            P(),
            P(None, None, "tensor"),
            P(None, "tensor"),
            P("tensor", None),
            P(),
            P(),
            P(),
            P(None, "tensor"),
            P("tensor"),
            P("tensor", None),
            P(),
            P(("dp", "tensor"), None),
        ),
        out_specs=(
            P(("dp", "tensor"), None),
            P(("dp", "tensor"), None),
            P(),
            P(),
            P(None, None, "tensor"),
            P(None, "tensor"),
            P("tensor", None),
            P(),
            P(),
            P(),
            P(None, "tensor"),
            P("tensor"),
            P("tensor", None),
            P(),
        ),
        check_vma=False,
    )
```

profile of v0, /device:TPU:0, one launch (start us, length us, event | category | flops | bytes accessed | tf_op | source)
XLA Modules:
  0.0 774.6 jit_solution(3344573649310132532)
XLA Ops:
  12.9 31.1 %all-gather.5.cloned.1.call-done = bf16[2048,768]{1,0:T(8,128)(2,1)} async-done(((bf16[512,768]{1,0:T(8,128)(2,1)}), bf16[2048,768]{1,0:T(8,128)(2,1)}) %all-gather.5.cloned.1.call-update) | async-done | bytes 3145744 | tf_op jit(solution)/shard_map/all_gather | solution.py:122
  62.2 27.5 %while.26 = (s32[]{:T(128)}, bf16[2,1024,3,64]{1,3,2,0:T(8,128)(2,1)}, f32[2,3,1024]{2,1,0:T(4,128)}, bf16[2,1024,3,64]{1,3,2,0:T(8,128)(2,1)S(1)}, s32[2,1024]{...) while((s32[]{:T(128)}, ...), condition=%wide.region_7.8_spmd, body=%wide.region_2.7_spmd.sunk | while | flops 846987264 | bytes 51563212 | solution.py:127
  96.8 58.4 %reduce-scatter.5.cloned.1.call-done = f32[512,768]{1,0:T(8,128)} async-done(((f32[2048,768]{1,0:T(8,128)}), f32[512,768]{1,0:T(8,128)}) %reduce-scatter.5.cloned.1.call-update) | async-done | bytes 1572880 | tf_op jit(solution)/shard_map/reduce_scatter | solution.py:131
  160.0 28.1 %all-gather.7.cloned.1.call-done = bf16[2048,768]{1,0:T(8,128)(2,1)} async-done(((bf16[512,768]{1,0:T(8,128)(2,1)}), bf16[2048,768]{1,0:T(8,128)(2,1)}) %all-gather.7.cloned.1.call-update) | async-done | bytes 3145744 | tf_op jit(solution)/shard_map/all_gather | solution.py:144
  188.0 7.5 fusion.121
  195.6 22.6 %all-gather.9.cloned.1.call-done = bf16[2048,768]{1,0:T(8,128)(2,1)} async-done(((bf16[512,768]{1,0:T(8,128)(2,1)}), bf16[2048,768]{1,0:T(8,128)(2,1)}) %all-gather.9.cloned.1.call-update) | async-done | bytes 3145744 | tf_op jit(solution)/shard_map/all_gather | solution.py:162
  218.1 12.4 %convert_reduce_fusion = (f32[768]{0:T(1024)}, bf16[2048,768]{1,0:T(8,128)(2,1)S(1)}, bf16[2048,768]{1,0:T(8,128)(2,1)}) fusion(f32[2048,768]{1,0:T(8,128)} %fusion.121, f32[768]{0:T(1024)S(1)} %copy-done.59, bf16[2048,768]{1,0:T(8,128)(2,1)} %all-gather.9.cloned.1.call-done, bf16[768,768]{1,0:T(8,128)(2,1)S(1)} %copy-done), kind=kOutput, calls=%fused_computation.122 | convolution fusion | flops 2455239936 | bytes 16914432 | tf_op jit(solution)/shard_map/dot_general | solution.py:165
  232.2 4.6 fusion.122
  236.9 6.5 convolution_convert_fusion
  243.5 51.9 %reduce-scatter.9.cloned.1.call-done = f32[512,768]{1,0:T(8,128)} async-done(((f32[2048,768]{1,0:T(8,128)}), f32[512,768]{1,0:T(8,128)}) %reduce-scatter.9.cloned.1.call-update) | async-done | bytes 1572880 | tf_op jit(solution)/shard_map/reduce_scatter | solution.py:174
  298.4 37.3 %reduce-scatter.7.cloned.1.call-done = bf16[512,768]{1,0:T(8,128)(2,1)} async-done(((bf16[2048,768]{1,0:T(8,128)(2,1)}), bf16[512,768]{1,0:T(8,128)(2,1)}) %reduce-scatter.7.cloned.1.call-update) | async-done | bytes 786448 | tf_op jit(solution)/shard_map/reduce_scatter | solution.py:149
  341.8 28.6 %all-gather.11.cloned.1.call-done = bf16[2048,768]{1,0:T(8,128)(2,1)} async-done(((bf16[512,768]{1,0:T(8,128)(2,1)}), bf16[2048,768]{1,0:T(8,128)(2,1)}) %all-gather.11.cloned.1.call-update) | async-done | bytes 3145744 | tf_op jit(solution)/shard_map/all_gather | solution.py:190
  381.0 67.5 %while.27 = (s32[]{:T(128)}, bf16[2,1024,3,64]{1,3,2,0:T(8,128)(2,1)}, bf16[2,1024,3,64]{1,3,2,0:T(8,128)(2,1)}, bf16[2,1024,3,64]{1,3,2,0:T(8,128)(2,1)}, bf16[...) while((s32[]{:T(128)}, ...), condition=%wide.region_18.19_spmd, body=%wide.region_15.18_spmd.sunk | while | flops 2065363968 | bytes 152608768 | solution.py:200
  388.6 4.4 multiply_reduce_fusion.7
  392.9 4.4 multiply_reduce_fusion.8
  397.3 7.7 multiply_convert_fusion.4
  426.5 4.4 multiply_reduce_fusion.8
  430.8 7.7 multiply_convert_fusion.4
  455.7 4.6 convolution_bitcast_fusion
  460.3 7.1 fusion.125
  480.3 22.0 %all-reduce.1 = (f32[2,192]{1,0:T(2,128)}, f32[768]{0:T(1024)}) all-reduce(f32[2,192]{1,0:T(2,128)S(1)} %pad_maximum_fusion, f32[768]{0:T(1024)S(1)} %copy-done.52), channel_id=1, replica_groups=mesh['dp'=8,'tensor'=4] {'dp'}, use_global_device_ids=true, to_apply=%region_29.30 | all-reduce | flops 1152 | bytes 9216 | tf_op jit(solution)/shard_map/psum | solution.py:221
  502.3 16.5 %reduce-scatter.11.cloned.1.call-done = f32[512,768]{1,0:T(8,128)} async-done(((f32[2048,768]{1,0:T(8,128)}), f32[512,768]{1,0:T(8,128)}) %reduce-scatter.11.cloned.1.call-update) | async-done | bytes 1572880 | tf_op jit(solution)/shard_map/reduce_scatter | solution.py:212
  523.7 43.8 %all-reduce = (f32[768]{0:T(1024)}, f32[768]{0:T(1024)}, f32[768]{0:T(1024)}, f32[768]{0:T(1024)}, f32[768]{0:T(1024)}, /*index=5*/f32[768]{0:T(1024)}) all-reduce(f32[768]{0:T(1024)S(1)} %get-tuple-element.147, f32[768]{0:T(1024)S(1)} %get-tuple-element.150, ...), channel_id=1, replica_groups=mesh['dp'=8,'tensor'=4] {'dp','tensor'}, use_global_device_ids=true, to_apply=%region_23.24 | all-reduce | flops 4608 | bytes 36864 | tf_op jit(solution)/shard_map/psum | solution.py:224
  567.5 193.8 %all-reduce.5.cloned.1.call-done = (f32[768,3,192]{0,2,1:T(8,128)}, f32[192,768]{1,0:T(8,128)}, f32[768,768]{1,0:T(8,128)}, f32[768,768]{1,0:T(8,128)}) async-done(((f32[768,3,192]{0,2,1:T(8,128)}, f32[192,768]{1,0:T(8,128)}, f32[768,768]{1,0:T(8,128)}, f32[768,768]{1,0:T(8,128)}), (f32[768,3,192]{0,2,1:T(8,128)}, f32[192,768]{1,0:T(8,128)}, f32[768,768]{1,0:T(8,128)}, ...) | async-done | bytes 7077904 | tf_op jit(solution)/shard_map/psum | solution.py:221
  (300 shorter events, 153.5 us)
Async XLA Ops:
  7.2 210.9 %copy-start = (bf16[768,768]{1,0:T(8,128)(2,1)S(1)}, bf16[768,768]{1,0:T(8,128)(2,1)}, u32[]{:S(2)}) copy-start(bf16[768,768]{1,0:T(8,128)(2,1)} %param.31) | copy-start | bytes 3538948
  7.2 36.8 %all-gather.5.cloned.1.call-start = ((), (), s32[]{:S(2)}) async-start(), calls=%async_computation.4 | async-start | bytes 3932160 | tf_op jit(solution)/shard_map/all_gather | solution.py:122
  12.7 142.6 %reduce-scatter.5.cloned.1.call-start = ((), (), s32[]{:S(2)}) async-start(), calls=%async_computation.5 | async-start | bytes 7864320 | tf_op jit(solution)/shard_map/reduce_scatter | solution.py:131
  96.7 58.5 %copy-start.6 = (bf16[512,768]{1,0:T(8,128)(2,1)S(1)}, bf16[512,768]{1,0:T(8,128)(2,1)}, u32[]{:S(2)}) copy-start(bf16[512,768]{1,0:T(8,128)(2,1)} %param.19) | copy-start | bytes 2359300
  96.8 61.4 %copy-start.41 = (f32[768]{0:T(1024)S(1)}, f32[768]{0:T(1024)}, u32[]{:S(2)}) copy-start(f32[768]{0:T(1024)} %param.27) | copy-start | bytes 9220
  96.8 61.4 %copy-start.50 = (f32[768]{0:T(1024)S(1)}, f32[768]{0:T(1024)}, u32[]{:S(2)}) copy-start(f32[768]{0:T(1024)} %param.28) | copy-start | bytes 9220
  96.8 91.3 %all-gather.7.cloned.1.call-start = ((), (), s32[]{:S(2)}) async-start(), calls=%async_computation.6 | async-start | bytes 3932160 | tf_op jit(solution)/shard_map/all_gather | solution.py:144
  159.4 58.8 %all-gather.9.cloned.1.call-start = ((), (), s32[]{:S(2)}) async-start(), calls=%async_computation.8 | async-start | bytes 3932160 | tf_op jit(solution)/shard_map/all_gather | solution.py:162
  159.9 58.2 %copy-start.59 = (f32[768]{0:T(1024)S(1)}, f32[768]{0:T(1024)}, u32[]{:S(2)}) copy-start(f32[768]{0:T(1024)} %param.30) | copy-start | bytes 9220
  159.9 135.4 %reduce-scatter.9.cloned.1.call-start = ((), (), s32[]{:S(2)}) async-start(), calls=%async_computation.9 | async-start | bytes 7864320 | tf_op jit(solution)/shard_map/reduce_scatter | solution.py:174
  236.8 98.9 %reduce-scatter.7.cloned.1.call-start = ((), (), s32[]{:S(2)}) async-start(), calls=%async_computation.7 | async-start | bytes 3932160 | tf_op jit(solution)/shard_map/reduce_scatter | solution.py:149
  243.4 92.3 %copy-start.51 = (f32[768]{0:T(1024)S(1)}, f32[768]{0:T(1024)}, u32[]{:S(2)}) copy-start(f32[768]{0:T(1024)} %param.32) | copy-start | bytes 9220
  243.4 127.0 %all-gather.11.cloned.1.call-start = ((), (), s32[]{:S(2)}) async-start(), calls=%async_computation.10 | async-start | bytes 3932160 | tf_op jit(solution)/shard_map/all_gather | solution.py:190
  298.4 42.1 %copy-start.17 = (bf16[512,768]{1,0:T(8,128)(2,1)S(1)}, bf16[512,768]{1,0:T(8,128)(2,1)}, u32[]{:S(2)}) copy-start(bf16[512,768]{1,0:T(8,128)(2,1)} %param.33) | copy-start | bytes 2359300
  341.7 177.1 %reduce-scatter.11.cloned.1.call-start = ((), (), s32[]{:S(2)}) async-start(), calls=%async_computation.11 | async-start | bytes 7864320 | tf_op jit(solution)/shard_map/reduce_scatter | solution.py:212
  460.3 301.0 %all-reduce.5.cloned.1.call-start = ((), (), s32[]{:S(2)}) async-start(), calls=%async_computation.12 | async-start | bytes 14155776 | tf_op jit(solution)/shard_map/psum | solution.py:221
  477.2 41.6 %copy-start.7 = (bf16[512,768]{1,0:T(8,128)(2,1)S(1)}, bf16[512,768]{1,0:T(8,128)(2,1)}, u32[]{:S(2)}) copy-start(bf16[512,768]{1,0:T(8,128)(2,1)} %param.19) | copy-start | bytes 2359300
  477.2 41.6 %copy-start.39 = (f32[512]{0:T(512)S(1)}, f32[512]{0:T(512)}, u32[]{:S(2)}) copy-start(f32[512]{0:T(512)} %copy-done.38) | copy-start | bytes 6148
  477.2 41.6 %copy-start.40 = (f32[768]{0:T(1024)S(1)}, f32[768]{0:T(1024)}, u32[]{:S(2)}) copy-start(f32[768]{0:T(1024)} %param.21) | copy-start | bytes 9220
  477.3 43.5 %copy-start.47 = (f32[512]{0:T(512)S(1)}, f32[512]{0:T(512)}, u32[]{:S(2)}) copy-start(f32[512]{0:T(512)} %copy-done.46) | copy-start | bytes 6148
  477.3 43.5 %copy-start.43 = (f32[512]{0:T(512)S(1)}, f32[512]{0:T(512)}, u32[]{:S(2)}) copy-start(f32[512]{0:T(512)} %copy-done.42) | copy-start | bytes 6148
  477.3 44.4 %copy-start.13 = (f32[512,768]{1,0:T(8,128)S(1)}, f32[512,768]{1,0:T(8,128)}, u32[]{:S(2)}) copy-start(f32[512,768]{1,0:T(8,128)} %copy-done.12) | copy-start | bytes 4718596
  477.3 44.4 %copy-start.18 = (bf16[512,768]{1,0:T(8,128)(2,1)S(1)}, bf16[512,768]{1,0:T(8,128)(2,1)}, u32[]{:S(2)}) copy-start(bf16[512,768]{1,0:T(8,128)(2,1)} %param.33) | copy-start | bytes 2359300
  477.3 44.4 %copy-start.45 = (f32[512]{0:T(512)S(1)}, f32[512]{0:T(512)}, u32[]{:S(2)}) copy-start(f32[512]{0:T(512)} %copy-done.44) | copy-start | bytes 6148
  (60 other events, 382.0 us)
Sparse Core Ops, SparseCore 0:
  12.8 31.2 all-gather.4
  96.9 58.3 reduce-scatter.4
  159.5 28.5 all-gather.6
  189.5 28.5 all-gather.8
  236.9 58.3 reduce-scatter.8
  297.7 37.9 reduce-scatter.6
  341.8 28.5 all-gather.10
  460.4 58.3 reduce-scatter.10
  524.4 236.8 all-reduce.4
where the time goes:
time: 778 us; the launch traced here: 775 us
  waiting for transfers between devices  469 us (60%)
  matrix products  121 us (16%)
  blocking collectives  65.8 us (8%)
  other arithmetic  54.8 us (7%)
  local copies, waits for them, and re-layouts  47.9 us (6%)
  between operations  14.6 us (2%)
    psum x1, waiting for transfers between devices, on_device(): lax.psum((d_w_qkv, d_b_qv, d_w_out, d_w_fc, d_b_fc, d_w_proj), 'dp')  194 us
    reduce_scatter x1, waiting for transfers between devices, on_device(): lax.psum_scatter(jnp.dot(lax.slice_in_dim(mixed_heads, 0, row_count * lax...  58.4 us
    reduce_scatter x1, waiting for transfers between devices, on_device(): lax.psum_scatter(jnp.dot(lax.slice_in_dim(grad_pre, 0, row_count * lax.ax...  51.9 us
    psum x1, blocking collectives, on_device(): lax.psum((d_ln1_gain, d_ln1_bias, d_b_out, d_ln2_gain, d_ln2_bias, d_b_pr...  43.8 us
    reduce_scatter x1, waiting for transfers between devices, on_device(): lax.psum_scatter(jnp.dot(lax.slice_in_dim(hidden, 0, row_count * lax.axis...  37.3 us
    all_gather x1, waiting for transfers between devices, on_device(): normed_all = lax.all_gather(normed, 'tensor', axis=0, tiled=True)  31.1 us
    all_gather x1, waiting for transfers between devices, on_device(): shard_rows = lax.all_gather(resid_low, 'tensor', axis=0, tiled=True)  28.6 us
    all_gather x1, waiting for transfers between devices, on_device(): normed2_all = lax.all_gather(normed2, 'tensor', axis=0, tiled=True)  28.1 us
  transfers between devices with their start and end apart: 9, of which 9 were waited for; matrix products, arithmetic and copies ran while one was open for 5% of the time, Pallas kernels for 0%

commit v1 on v0

v1 whole, which is shorter than its diff:
```python
import functools

import jax
import jax.numpy as jnp
from jax import lax
from jax.experimental import pallas as pl
from jax.experimental.pallas import tpu as pltpu
from jax.sharding import PartitionSpec as P

HD = 64
LANES = 128
NEG_FILL = -1e30
SCALE = HD ** (-0.5)
F32 = jnp.float32
BF16 = jnp.bfloat16

NT = (((1,), (1,)), ((), ()))
TN = (((0,), (0,)), ((), ()))
NN = (((1,), (0,)), ((), ()))


def mm(a, b, dims=NN):
    return lax.dot_general(a, b, dims, preferred_element_type=F32)


def layer_norm(values, norm_gain, norm_shift):
    center = values - jnp.mean(values, -1, keepdims=True)
    variance = jnp.mean(center * center, -1, keepdims=True)
    return center * lax.rsqrt(variance + 1e-05) * norm_gain + norm_shift


def head_lanes(shape, head):
    lane = lax.broadcasted_iota(jnp.int32, shape, 1)
    return (lane // HD) == head


def only_head(values, head):
    return jnp.where(head_lanes(values.shape, head), values, jnp.zeros_like(values))


def attend_kernel(q_ref, k_ref, v_ref, bias_ref, mixed_ref, lse_ref):
    queries, keys, values = q_ref[...], k_ref[...], v_ref[...]
    mixed = jnp.zeros(queries.shape, F32)
    lse = jnp.zeros(queries.shape, F32)
    for head in range(LANES // HD):
        scores = mm(only_head(queries, head), keys, NT) * SCALE + bias_ref[0]
        top = jnp.max(scores, -1, keepdims=True)
        expo = jnp.exp(scores - top)
        total = jnp.sum(expo, -1, keepdims=True)
        probs = (expo * (1.0 / total)).astype(BF16)
        mine = head_lanes(queries.shape, head)
        mixed = jnp.where(mine, mm(probs, values), mixed)
        lse = jnp.where(mine, top + jnp.log(total), lse)
    mixed_ref[...] = mixed.astype(BF16)
    lse_ref[...] = lse


def attend_back_kernel(q_ref, k_ref, v_ref, bias_ref, g_ref, lse_ref, dq_ref, dk_ref, dv_ref):
    queries, keys, values, grad = q_ref[...], k_ref[...], v_ref[...], g_ref[...]
    dq = jnp.zeros(queries.shape, F32)
    dk = jnp.zeros(keys.shape, F32)
    dv = jnp.zeros(keys.shape, F32)
    for head in range(LANES // HD):
        scores = mm(only_head(queries, head), keys, NT) * SCALE + bias_ref[0]
        probs = jnp.exp(scores - lse_ref[:, head * HD : head * HD + 1])
        grad_probs = mm(only_head(grad, head), values, NT)
        inner = jnp.sum(probs * grad_probs, -1, keepdims=True)
        grad_scores = (probs * (grad_probs - inner)).astype(BF16)
        dq = jnp.where(head_lanes(dq.shape, head), mm(grad_scores, keys), dq)
        dk = jnp.where(head_lanes(dk.shape, head), mm(grad_scores, queries, TN), dk)
        dv = jnp.where(head_lanes(dv.shape, head), mm(probs.astype(BF16), grad, TN), dv)
    dq_ref[...] = (dq * SCALE).astype(BF16)
    dk_ref[...] = (dk * SCALE).astype(BF16)
    dv_ref[...] = dv.astype(BF16)


def attention_call(kernel, bias, arrays, out_types, matmuls, kinds, out_kinds):
    seqs, qlen, klen = bias.shape
    width = arrays[0].shape[1]
    pairs = width // LANES
    spec = {
        "q": pl.BlockSpec((qlen, LANES), lambda s, p: (s, p)),
        "k": pl.BlockSpec((klen, LANES), lambda s, p: (s, p)),
        "b": pl.BlockSpec((1, qlen, klen), lambda s, p: (s, 0, 0)),
    }
    rows = {"q": seqs * qlen, "k": seqs * klen}
    area = seqs * qlen * klen * (width // HD)
    return pl.pallas_call(
        kernel,
        grid=(seqs, pairs),
        in_specs=[spec[kind] for kind in kinds],
        out_specs=[spec[kind] for kind in out_kinds],
        out_shape=[
            jax.ShapeDtypeStruct((rows[kind], width), dtype)
            for kind, dtype in zip(out_kinds, out_types)
        ],
        compiler_params=pltpu.CompilerParams(vmem_limit_bytes=48 * 1024 * 1024),
        cost_estimate=pl.CostEstimate(
            flops=2 * HD * area * matmuls * 4, bytes_accessed=8 * rows["k"] * width, transcendentals=area
        ),
    )(*arrays)


def swap(values, bit, axis="tensor"):
    size = lax.axis_size(axis)
    return lax.ppermute(values, axis, [(i, i ^ bit) for i in range(size)])


def bits_of(count):
    bit, found = 1, []
    while bit < count:
        found.append(bit)
        bit *= 2
    return found


def gather_pieces(own, count):
    pieces = {0: own}
    for bit in reversed(bits_of(count)):
        for j in list(pieces):
            pieces[j ^ bit] = swap(pieces[j], bit)
    return [pieces[j] for j in range(count)]


def reduce_pieces(pieces):
    held = dict(enumerate(pieces))
    for bit in bits_of(len(pieces)):
        held = {
            j: held[j] + swap(held[j ^ bit].astype(BF16), bit).astype(F32)
            for j in held
            if not j & bit
        }
    return held[0]


def reorder(pieces, me, span):
    for bit in bits_of(span):
        odd = (me & bit) != 0
        pieces = [jnp.where(odd, pieces[c ^ bit], pieces[c]) for c in range(len(pieces))]
    return pieces


def split_rows(values, count):
    step = values.shape[0] // count
    return [values[c * step : (c + 1) * step] for c in range(count)]


def on_device(
    tokens,
    segment_ids,
    ln1_gain,
    ln1_bias,
    w_qkv,
    b_qv,
    w_out,
    b_out,
    ln2_gain,
    ln2_bias,
    w_fc,
    b_fc,
    w_proj,
    b_proj,
    cotangent,
):
    count = lax.axis_size("tensor")
    me = lax.axis_index("tensor")
    rows, width = tokens.shape
    seq_len = segment_ids.shape[1]
    local = w_qkv.shape[2]
    span = max(seq_len // rows, 1)
    seqs = max(rows // seq_len, 1)
    qlen = rows // seqs

    own_qkv = w_qkv.transpose(1, 2, 0).reshape(3 * local, width)
    own_bias = jnp.concatenate([b_qv.reshape(-1), b_fc])
    biases = gather_pieces(own_bias, count)
    qkv = reorder(gather_pieces(own_qkv, count), me, span)
    outs = reorder(gather_pieces(w_out, count), me, span)
    fcs = gather_pieces(w_fc, count)
    projs = gather_pieces(w_proj, count)
    bqv = reorder([b[: 2 * local] for b in biases], me, span)
    bfc = [b[2 * local :] for b in biases]
    wq, wk, wv = [
        jnp.concatenate([piece[c * local : (c + 1) * local] for piece in qkv], 0) for c in range(3)
    ]
    bq, bv = [
        jnp.concatenate([piece[c * local : (c + 1) * local] for piece in bqv], 0) for c in range(2)
    ]
    wo = jnp.concatenate(outs, 0)

    first = me * rows // seq_len
    own_segs = lax.dynamic_slice_in_dim(segment_ids, first, seqs, 0)
    starts = [((me ^ o) * rows) % seq_len for o in range(span)]
    parts = [lax.dynamic_slice_in_dim(own_segs, start, qlen, 1) for start in starts]
    places = [start + jnp.arange(qlen) for start in starts]
    key_seg, key_pos = jnp.concatenate(parts, 1), jnp.concatenate(places, 0)
    allowed = (key_pos[None, None, :] <= places[0][None, :, None]) & (
        key_seg[:, None, :] == parts[0][:, :, None]
    )
    mask = jnp.where(allowed, 0.0, NEG_FILL).astype(F32)

    x_full = tokens.astype(F32)
    normed = layer_norm(x_full, ln1_gain, ln1_bias).astype(BF16)
    keys = mm(normed, wk, NT).astype(BF16)
    values = (mm(normed, wv, NT) + bv).astype(BF16)
    keys = jnp.concatenate([keys] + [swap(keys, o) for o in range(1, span)], 0)
    values = jnp.concatenate([values] + [swap(values, o) for o in range(1, span)], 0)
    queries = (mm(normed, wq, NT) + bq).astype(BF16)
    mixed, lse = attention_call(
        attend_kernel, mask, (queries, keys, values, mask), (BF16, F32), 2, "qkkb", "qq"
    )
    residual = x_full + mm(mixed, wo) + b_out
    normed2 = layer_norm(residual, ln2_gain, ln2_bias).astype(BF16)

    gelu = functools.partial(jax.nn.gelu, approximate=True)
    result = residual + b_proj
    d_proj, d_fc, d_bfc = [], [], []
    grad_normed2 = jnp.zeros((rows, width), F32)
    for j in range(count):
        pre_act = mm(normed2, fcs[j]) + bfc[j]
        hidden, gelu_back = jax.vjp(gelu, pre_act)
        hidden = hidden.astype(BF16)
        result = result + mm(hidden, projs[j])
        d_proj.append(mm(hidden, cotangent, TN))
        grad_pre = gelu_back(mm(cotangent, projs[j], NT))[0].astype(BF16)
        d_bfc.append(jnp.sum(grad_pre.astype(F32), 0))
        d_fc.append(mm(normed2, grad_pre, TN))
        grad_normed2 = grad_normed2 + mm(grad_pre, fcs[j], NT)
    output = result.astype(BF16)
    g_proj = lax.psum(reduce_pieces(d_proj).astype(BF16), "dp")
    own_fc, g_proj = lax.optimization_barrier((reduce_pieces(d_fc).astype(BF16), g_proj))
    g_fc = lax.psum(own_fc, "dp")

    cot_full = cotangent.astype(F32)
    _, ln2_back = jax.vjp(layer_norm, residual, ln2_gain, ln2_bias)
    grad_resid_part, d_ln2_gain, d_ln2_bias = ln2_back(grad_normed2)
    grad_resid = cot_full + grad_resid_part
    d_b_proj = jnp.sum(cot_full, 0)
    d_b_out = jnp.sum(grad_resid, 0)
    resid_low = grad_resid.astype(BF16)
    grad_mixed = mm(resid_low, wo, NT).astype(BF16)
    d_out = split_rows(mm(mixed, resid_low, TN), count)
    dq, dk, dv = attention_call(
        attend_back_kernel,
        mask,
        (queries, keys, values, mask, grad_mixed, lse),
        (BF16, BF16, BF16),
        5,
        "qkkbqq",
        "qkk",
    )
    if span > 1:
        dk, dv = [
            sum(
                [swap(grad[o * rows : (o + 1) * rows], o).astype(F32) for o in range(1, span)],
                grad[:rows].astype(F32),
            ).astype(BF16)
            for grad in (dk, dv)
        ]
    d_packed = [split_rows(mm(grad, normed, TN), count) for grad in (dq, dk, dv)]
    d_attn = [
        jnp.concatenate([d_packed[0][c], d_packed[1][c], d_packed[2][c], d_out[c]], 0)
        for c in range(count)
    ]
    own_attn = reduce_pieces(reorder(d_attn, me, span)).astype(BF16)
    own_attn, g_fc = lax.optimization_barrier((own_attn, g_fc))
    g_attn = lax.psum(own_attn, "dp")
    d_bq = split_rows(jnp.sum(dq.astype(F32), 0), count)
    d_bv = split_rows(jnp.sum(dv.astype(F32), 0), count)
    d_bqv = reorder([jnp.concatenate([d_bq[c], d_bv[c]]) for c in range(count)], me, span)

    grad_normed = mm(dq, wq) + mm(dk, wk) + mm(dv, wv)
    _, ln1_back = jax.vjp(layer_norm, x_full, ln1_gain, ln1_bias)
    grad_tok_part, d_ln1_gain, d_ln1_bias = ln1_back(grad_normed)
    d_tokens = grad_resid + grad_tok_part

    shared = jnp.stack([d_ln1_gain, d_ln1_bias, d_b_out, d_ln2_gain, d_ln2_bias, d_b_proj])
    held = {j: jnp.concatenate([d_bqv[j], d_bfc[j]]) for j in range(count)}
    for bit in bits_of(count):
        send = jnp.concatenate([held[j] for j in held if j & bit] + [shared.reshape(-1)])
        got = swap(send, bit)
        keep = [j for j in held if not j & bit]
        size = held[0].shape[0]
        order = [j ^ bit for j in held if j & bit]
        held = {
            j: held[j] + got[order.index(j) * size : (order.index(j) + 1) * size] for j in keep
        }
        shared = shared + got[len(order) * size :].reshape(shared.shape)
    small = jnp.concatenate([held[0], shared.reshape(-1)])
    for bit in bits_of(lax.axis_size("dp")):
        small = small + swap(small, bit, "dp")
    d_b_qv = small[: 2 * local].reshape(2, local)
    d_b_fc = small[2 * local : held[0].shape[0]]
    shared = small[held[0].shape[0] :].reshape(shared.shape)

    d_w_qkv = g_attn[: 3 * local].astype(F32).reshape(3, local, width).transpose(2, 0, 1)
    d_w_out = g_attn[3 * local :].astype(F32)
    return (
        output,
        d_tokens,
        shared[0],
        shared[1],
        d_w_qkv,
        d_b_qv,
        d_w_out,
        shared[2],
        shared[3],
        shared[4],
        g_fc.astype(F32),
        d_b_fc,
        g_proj.astype(F32),
        shared[5],
    )


def solution(mesh):
    return jax.shard_map(
        on_device,
        mesh=mesh,
        in_specs=(
            P(("dp", "tensor"), None),
            P("dp", None),
            P(),
            P(),
            P(None, None, "tensor"),
            P(None, "tensor"),
            P("tensor", None),
            P(),
            P(),
            P(),
            P(None, "tensor"),
            P("tensor"),
            P("tensor", None),
            P(),
            P(("dp", "tensor"), None),
        ),
        out_specs=(
            P(("dp", "tensor"), None),
            P(("dp", "tensor"), None),
            P(),
            P(),
            P(None, None, "tensor"),
            P(None, "tensor"),
            P("tensor", None),
            P(),
            P(),
            P(),
            P(None, "tensor"),
            P("tensor"),
            P("tensor", None),
            P(),
        ),
        check_vma=False,
    )
```

time: 778 us -> 511 us (0.66)
  waiting for transfers between devices: 469 us -> 282 us
  blocking collectives: 65.8 us -> 0 us
  matrix products: 121 us -> 63.6 us
  Pallas kernels: 0 us -> 44.3 us
  local copies, waits for them, and re-layouts: 47.9 us -> 26.9 us
  starting transfers between devices: 0.37 us -> 17.8 us
    reduce_scatter x4 -> x0, waiting for transfers between devices: 164 us -> none  [the longest x1 58.4 us: on_device(): lax.psum_scatter(jnp.dot(lax.slice_in_dim(mixed_heads, 0, row_count * lax...]
    all_gather x4 -> x0, waiting for transfers between devices: 110 us -> none  [the longest x1 31.1 us: on_device(): normed_all = lax.all_gather(normed, 'tensor', axis=0, tiled=True)]
    ppermute x0 -> x33, waiting for transfers between devices: none -> 85.8 us  [swap(): return lax.ppermute(values, axis, [(i, i ^ bit) for i in range(size)])]
    psum x2 -> x0, blocking collectives: 65.8 us -> none  [the longest x1 43.8 us: on_device(): lax.psum((d_ln1_gain, d_ln1_bias, d_b_out, d_ln2_gain, d_ln2_bias, d_b_pr...]
    dot_general x38 -> x36, matrix products: 114 us -> 63.6 us  [mm(): return lax.dot_general(a, b, dims, preferred_element_type=F32)]
    pallas_call x0 -> x2, Pallas kernels: none -> 44.3 us  [attention_call(): pl.pallas_call(kernel, grid=(seqs, pairs), in_specs=[spec[kind] for kind...]
    ppermute x0 -> x33, starting transfers between devices: none -> 17.6 us  [swap(): return lax.ppermute(values, axis, [(i, i ^ bit) for i in range(size)])]
    reduce_sum x4 -> x2, other arithmetic: 9.79 us -> 0.39 us  [the longest x1 0.24 us: on_device(): d_bv = split_rows(jnp.sum(dv.astype(F32), 0), count)]
  transfers between devices with their start and end apart: 9 -> 36, of which waited for: 9 -> 10; matrix products, arithmetic and copies ran while one was open for 5% -> 20% of each run, Pallas kernels for 0% -> 3%
where the time goes in v1:
time: 511 us; the launch traced here: 503 us
  waiting for transfers between devices  282 us (55%)
  matrix products  63.6 us (12%)
  other arithmetic  53.1 us (10%)
  Pallas kernels  44.3 us (9%)
  local copies, waits for them, and re-layouts  26.9 us (5%)
  starting transfers between devices  17.8 us (3%)
  between operations  15.5 us (3%)
    ppermute x33, waiting for transfers between devices, swap(): return lax.ppermute(values, axis, [(i, i ^ bit) for i in range(size)])  85.8 us
    psum x1, waiting for transfers between devices, on_device(): g_fc = lax.psum(own_fc, 'dp')  71.7 us
    psum x1, waiting for transfers between devices, on_device(): g_attn = lax.psum(own_attn, 'dp')  69.5 us
    dot_general x36, matrix products, mm(): return lax.dot_general(a, b, dims, preferred_element_type=F32)  63.6 us
    psum x1, waiting for transfers between devices, on_device(): g_proj = lax.psum(reduce_pieces(d_proj).astype(BF16), 'dp')  54.6 us
    pallas_call x2, Pallas kernels, attention_call(): pl.pallas_call(kernel, grid=(seqs, pairs), in_specs=[spec[kind] for kind...  44.3 us
    ppermute x33, starting transfers between devices, swap(): return lax.ppermute(values, axis, [(i, i ^ bit) for i in range(size)])  17.6 us
    reduce_sum x2, other arithmetic, layer_norm(): center = values - jnp.mean(values, -1, keepdims=True)  14.3 us
  transfers between devices with their start and end apart: 36, of which 10 were waited for; matrix products, arithmetic and copies ran while one was open for 20% of the time, Pallas kernels for 3%

profile of v1, /device:TPU:0, one launch (start us, length us, event | category | flops | bytes accessed | tf_op | source)
XLA Modules:
  0.0 502.8 jit_solution(9920678559258845152)
XLA Ops:
  8.8 3.0 collective-permute-start.4
  16.9 3.2 fusion.96
  23.6 10.9 %collective-permute-done.1 = bf16[576,768]{1,0:T(8,128)(2,1)} collective-permute-done((bf16[576,768]{1,0:T(8,128)(2,1)}, bf16[576,768]{1,0:T(8,128)(2,1)}, u32[]{:S(2)}, u32[]{:S(2)}) %collective-permute-start.1) | collective-permute-done | bytes 884768 | tf_op jit(solution)/shard_map/ppermute | solution.py:106
  34.7 30.9 %collective-permute-done.9 = bf16[192,768]{1,0:T(8,128)(2,1)S(1)} collective-permute-done((bf16[192,768]{1,0:T(8,128)(2,1)S(1)}, bf16[192,768]{1,0:T(8,128)(2,1)S(1)}, u32[]{:S(2)}, u32[]{:S(2)}) %collective-permute-start.9) | collective-permute-done | bytes 294944 | tf_op jit(solution)/shard_map/ppermute | solution.py:106
  76.3 17.2 %collective-permute-done.13 = bf16[768,768]{1,0:T(8,128)(2,1)} collective-permute-done((bf16[768,768]{1,0:T(8,128)(2,1)}, bf16[768,768]{1,0:T(8,128)(2,1)}, u32[]{:S(2)}, u32[]{:S(2)}) %collective-permute-start.13) | collective-permute-done | bytes 1179680 | tf_op jit(solution)/shard_map/ppermute | solution.py:106
  95.8 17.4 %shard_map.254 = (bf16[512,768]{1,0:T(8,128)(2,1)S(1)}, f32[512,768]{1,0:T(8,128)S(1)}) custom-call(bf16[512,768]{1,0:T(8,128)(2,1)S(1)} %add_convert_fusion.11.q_ref, bf16[1024,768]{1,0:T(8,128)(2,1)S(1)} %pad_maximum_fusion.4.k_ref, bf16[1024,768]{1,0:T(8,128)(2,1)} %pad_maximum_fusion.5.v_ref, f32[1,512,1024]{2,1,0:T(8,128)} %and_select_fusion.bias_ref), custom_call_target="tpu_custom_call" | custom-call | flops 6442450944 | bytes 6291456 | tf_op jit(solution)/shard_map/pallas_call | solution.py:88
  118.6 3.4 convert_reduce_fusion.2
  124.1 3.4 convert_reduce_fusion.5
  130.5 2.9 convert_reduce_fusion.4
  138.7 13.0 %fusion.78 = (f32[512]{0:T(512)S(1)}, f32[512,768]{1,0:T(8,128)S(1)}) fusion(f32[512]{0:T(512)S(1)} %multiply_multiply_fusion.9, f32[512,768]{1,0:T(8,128)S(1)} %get-tuple-element.122, f32[512]{0:T(512)S(1)} %broadcast_multiply_fusion, f32[512]{0:T(512)S(1)} %fusion.47, f32[512,768]{1,0:T(8,128)S(1)} %get-tuple-element.124, f32[768]{0:T(1024)S(1)} %copy-done.70), kind=kLoop, calls=%fused_computation.178 | loop fusion | flops 2752000 | bytes 4729856 | tf_op jit(solution)/shard_map/transpose(jvp())/reduce_sum | solution.py:27
  153.5 27.0 %shard_map.255 = (bf16[512,768]{1,0:T(8,128)(2,1)S(1)}, bf16[1024,768]{1,0:T(8,128)(2,1)S(1)}, bf16[1024,768]{1,0:T(8,128)(2,1)S(1)}) custom-call(bf16[512,768]{1,0:T(8,128)(2,1)S(1)} %add_convert_fusion.11.q_ref, bf16[1024,768]{1,0:T(8,128)(2,1)} %copy-done, bf16[1024,768]{1,0:T(8,128)(2,1)} %pad_maximum_fusion.5.v_ref, ...), custom_call_target="tpu_custom_call" | custom-call | flops 16106127360 | bytes 6291456 | tf_op jit(solution)/shard_map/pallas_call | solution.py:88
  197.5 2.4 fusion.59
  225.9 3.6 add_convert_fusion.3
  231.0 11.1 %collective-permute-done.32 = bf16[768,768]{1,0:T(8,128)(2,1)} collective-permute-done((bf16[768,768]{1,0:T(8,128)(2,1)}, bf16[768,768]{1,0:T(8,128)(2,1)}, u32[]{:S(2)}, u32[]{:S(2)}) %collective-permute-start.32) | collective-permute-done | bytes 1179680 | tf_op jit(solution)/shard_map/ppermute | solution.py:106
  242.0 3.2 add_convert_fusion
  246.3 3.2 select_convert_fusion.1
  254.0 13.3 %collective-permute-done.29 = bf16[768,768]{1,0:T(8,128)(2,1)} collective-permute-done((bf16[768,768]{1,0:T(8,128)(2,1)}, bf16[768,768]{1,0:T(8,128)(2,1)}, u32[]{:S(2)}, u32[]{:S(2)}) %collective-permute-start.29) | collective-permute-done | bytes 1179680 | tf_op jit(solution)/shard_map/ppermute | solution.py:106
  267.3 3.8 add_convert_fusion.2
  271.1 54.6 %all-reduce.4.cloned.1.call-done = bf16[768,768]{1,0:T(8,128)(2,1)} async-done(((bf16[768,768]{1,0:T(8,128)(2,1)}), bf16[768,768]{1,0:T(8,128)(2,1)}) %all-reduce.4.cloned.1.call-update) | async-done | bytes 1179664 | tf_op jit(solution)/shard_map/psum | solution.py:230
  327.3 4.0 fusion.63
  333.6 3.8 add_convert_fusion.4
  337.4 71.7 %all-reduce.6.cloned.1.call-done = bf16[768,768]{1,0:T(8,128)(2,1)} async-done(((bf16[768,768]{1,0:T(8,128)(2,1)}), bf16[768,768]{1,0:T(8,128)(2,1)}) %all-reduce.6.cloned.1.call-update) | async-done | bytes 1179664 | tf_op jit(solution)/shard_map/psum | solution.py:232
  410.3 3.4 fusion.61
  423.1 69.5 %all-reduce.8.cloned.1.call-done = bf16[768,768]{1,0:T(8,128)(2,1)} async-done(((bf16[768,768]{1,0:T(8,128)(2,1)}), bf16[768,768]{1,0:T(8,128)(2,1)}) %all-reduce.8.cloned.1.call-update) | async-done | bytes 1179664 | tf_op jit(solution)/shard_map/psum | solution.py:267
  (379 shorter events, 107.9 us)
Async XLA Ops:
  7.2 318.5 %all-reduce.4.cloned.1.call-start = ((), (), s32[]{:S(2)}) async-start(), calls=%async_computation | async-start | bytes 2359296 | tf_op jit(solution)/shard_map/psum | solution.py:230
  11.7 22.8 %collective-permute-start.1 = (bf16[576,768]{1,0:T(8,128)(2,1)}, bf16[576,768]{1,0:T(8,128)(2,1)}, u32[]{:S(2)}, u32[]{:S(2)}) collective-permute-start(bf16[576,768]{1,0:T(8,128)(2,1)} %bitcast.56), channel_id=1, source_target_pairs={{0,2},{1,3},{2,0},{3,1},{4,6},{5,7},{6,4},{7,5},{8,10},{9,11},{10,... | collective-permute-start | bytes 2654216 | tf_op jit(solution)/shard_map/ppermute | solution.py:106
  11.8 54.1 %collective-permute-start = (bf16[576,768]{1,0:T(8,128)(2,1)}, bf16[576,768]{1,0:T(8,128)(2,1)S(1)}, u32[]{:S(2)}, u32[]{:S(2)}) collective-permute-start(bf16[576,768]{1,0:T(8,128)(2,1)} %bitcast.57), channel_id=1, source_target_pairs={{0,1},{1,0},{2,3},{3,2},{4,5},{5,4},{6,7},{7,6},{8,9},{9,8},{10,11... | collective-permute-start | bytes 2654216 | tf_op jit(solution)/shard_map/ppermute | solution.py:106
  12.3 63.5 %collective-permute-start.14 = (bf16[768,768]{1,0:T(8,128)(2,1)}, bf16[768,768]{1,0:T(8,128)(2,1)}, u32[]{:S(2)}, u32[]{:S(2)}) collective-permute-start(bf16[768,768]{1,0:T(8,128)(2,1)} %param.27), channel_id=1, source_target_pairs={{0,2},{1,3},{2,0},{3,1},{4,6},{5,7},{6,4},{7,5},{8,10},{9,11},{10,... | collective-permute-start | bytes 3538952 | tf_op jit(solution)/shard_map/ppermute | solution.py:106
  21.9 43.7 %collective-permute-start.9 = (bf16[192,768]{1,0:T(8,128)(2,1)S(1)}, bf16[192,768]{1,0:T(8,128)(2,1)S(1)}, u32[]{:S(2)}, u32[]{:S(2)}) collective-permute-start(bf16[192,768]{1,0:T(8,128)(2,1)S(1)} %copy-done.60), channel_id=1, source_target_pairs={{0,2},{1,3},{2,0},{3,1},{4,6},{5,7},{6,4},{7,5},{8,10},{9,11},{10,... | collective-permute-start | bytes 884744 | tf_op jit(solution)/shard_map/ppermute | solution.py:106
  23.4 50.5 %collective-permute-start.8 = (bf16[192,768]{1,0:T(8,128)(2,1)S(1)}, bf16[192,768]{1,0:T(8,128)(2,1)S(1)}, u32[]{:S(2)}, u32[]{:S(2)}) collective-permute-start(bf16[192,768]{1,0:T(8,128)(2,1)S(1)} %copy-done.60), channel_id=1, source_target_pairs={{0,1},{1,0},{2,3},{3,2},{4,5},{5,4},{6,7},{7,6},{8,9},{9,8},{10,11... | collective-permute-start | bytes 884744 | tf_op jit(solution)/shard_map/ppermute | solution.py:106
  34.5 33.9 %collective-permute-start.2 = (bf16[576,768]{1,0:T(8,128)(2,1)}, bf16[576,768]{1,0:T(8,128)(2,1)S(1)}, u32[]{:S(2)}, u32[]{:S(2)}) collective-permute-start(bf16[576,768]{1,0:T(8,128)(2,1)} %collective-permute-done.1), channel_id=1, source_target_pairs={{0,1},{1,0},{2,3},{3,2},{4,5},{5,4},{6,7},{7,6},{8,9},{9,8},{10,11... | collective-permute-start | bytes 2654216 | tf_op jit(solution)/shard_map/ppermute | solution.py:106
  65.6 27.9 %collective-permute-start.13 = (bf16[768,768]{1,0:T(8,128)(2,1)}, bf16[768,768]{1,0:T(8,128)(2,1)}, u32[]{:S(2)}, u32[]{:S(2)}) collective-permute-start(bf16[768,768]{1,0:T(8,128)(2,1)} %param.25), channel_id=1, source_target_pairs={{0,2},{1,3},{2,0},{3,1},{4,6},{5,7},{6,4},{7,5},{8,10},{9,11},{10,... | collective-permute-start | bytes 3538952 | tf_op jit(solution)/shard_map/ppermute | solution.py:106
  74.3 56.2 %collective-permute-start.12 = (bf16[768,768]{1,0:T(8,128)(2,1)S(1)}, bf16[768,768]{1,0:T(8,128)(2,1)}, u32[]{:S(2)}, u32[]{:S(2)}) collective-permute-start(bf16[768,768]{1,0:T(8,128)(2,1)S(1)} %copy-done.82), channel_id=1, source_target_pairs={{0,1},{1,0},{2,3},{3,2},{4,5},{5,4},{6,7},{7,6},{8,9},{9,8},{10,11... | collective-permute-start | bytes 3538952 | tf_op jit(solution)/shard_map/ppermute | solution.py:106
  76.2 45.8 %collective-permute-start.11 = (bf16[768,768]{1,0:T(8,128)(2,1)S(1)}, bf16[768,768]{1,0:T(8,128)(2,1)S(1)}, u32[]{:S(2)}, u32[]{:S(2)}) collective-permute-start(bf16[768,768]{1,0:T(8,128)(2,1)S(1)} %copy-done.81), channel_id=1, source_target_pairs={{0,1},{1,0},{2,3},{3,2},{4,5},{5,4},{6,7},{7,6},{8,9},{9,8},{10,11... | collective-permute-start | bytes 3538952 | tf_op jit(solution)/shard_map/ppermute | solution.py:106
  93.5 41.6 %collective-permute-start.16 = (bf16[768,768]{1,0:T(8,128)(2,1)}, bf16[768,768]{1,0:T(8,128)(2,1)S(1)}, u32[]{:S(2)}, u32[]{:S(2)}) collective-permute-start(bf16[768,768]{1,0:T(8,128)(2,1)} %collective-permute-done.14), channel_id=1, source_target_pairs={{0,1},{1,0},{2,3},{3,2},{4,5},{5,4},{6,7},{7,6},{8,9},{9,8},{10,11... | collective-permute-start | bytes 3538952 | tf_op jit(solution)/shard_map/ppermute | solution.py:106
  93.5 40.8 %collective-permute-start.15 = (bf16[768,768]{1,0:T(8,128)(2,1)}, bf16[768,768]{1,0:T(8,128)(2,1)S(1)}, u32[]{:S(2)}, u32[]{:S(2)}) collective-permute-start(bf16[768,768]{1,0:T(8,128)(2,1)} %collective-permute-done.13), channel_id=1, source_target_pairs={{0,1},{1,0},{2,3},{3,2},{4,5},{5,4},{6,7},{7,6},{8,9},{9,8},{10,11... | collective-permute-start | bytes 3538952 | tf_op jit(solution)/shard_map/ppermute | solution.py:106
  196.8 29.1 %collective-permute-start.28 = (bf16[768,768]{1,0:T(8,128)(2,1)}, bf16[768,768]{1,0:T(8,128)(2,1)}, u32[]{:S(2)}, u32[]{:S(2)}) collective-permute-start(bf16[768,768]{1,0:T(8,128)(2,1)} %convolution_convert_fusion.2), channel_id=1, source_target_pairs={{0,1},{1,0},{2,3},{3,2},{4,5},{5,4},{6,7},{7,6},{8,9},{9,8},{10,11... | collective-permute-start | bytes 3538952 | tf_op jit(solution)/shard_map/ppermute | solution.py:106
  196.9 57.1 %collective-permute-start.27 = (bf16[768,768]{1,0:T(8,128)(2,1)}, bf16[768,768]{1,0:T(8,128)(2,1)}, u32[]{:S(2)}, u32[]{:S(2)}) collective-permute-start(bf16[768,768]{1,0:T(8,128)(2,1)} %convolution_convert_fusion.3), channel_id=1, source_target_pairs={{0,1},{1,0},{2,3},{3,2},{4,5},{5,4},{6,7},{7,6},{8,9},{9,8},{10,11... | collective-permute-start | bytes 3538952 | tf_op jit(solution)/shard_map/ppermute | solution.py:106
  200.0 29.5 %collective-permute-start.30 = (bf16[768,768]{1,0:T(8,128)(2,1)}, bf16[768,768]{1,0:T(8,128)(2,1)}, u32[]{:S(2)}, u32[]{:S(2)}) collective-permute-start(bf16[768,768]{1,0:T(8,128)(2,1)} %convolution_convert_fusion.1), channel_id=1, source_target_pairs={{0,1},{1,0},{2,3},{3,2},{4,5},{5,4},{6,7},{7,6},{8,9},{9,8},{10,11... | collective-permute-start | bytes 3538952 | tf_op jit(solution)/shard_map/ppermute | solution.py:106
  206.3 43.2 %collective-permute-start.25 = (bf16[768,768]{1,0:T(8,128)(2,1)}, bf16[768,768]{1,0:T(8,128)(2,1)}, u32[]{:S(2)}, u32[]{:S(2)}) collective-permute-start(bf16[768,768]{1,0:T(8,128)(2,1)} %select_convert_fusion), channel_id=1, source_target_pairs={{0,1},{1,0},{2,3},{3,2},{4,5},{5,4},{6,7},{7,6},{8,9},{9,8},{10,11... | collective-permute-start | bytes 3538952 | tf_op jit(solution)/shard_map/ppermute | solution.py:106
  212.9 29.1 %collective-permute-start.32 = (bf16[768,768]{1,0:T(8,128)(2,1)}, bf16[768,768]{1,0:T(8,128)(2,1)}, u32[]{:S(2)}, u32[]{:S(2)}) collective-permute-start(bf16[768,768]{1,0:T(8,128)(2,1)} %add_convert_fusion.1), channel_id=1, source_target_pairs={{0,2},{1,3},{2,0},{3,1},{4,6},{5,7},{6,4},{7,5},{8,10},{9,11},{10,... | collective-permute-start | bytes 3538952 | tf_op jit(solution)/shard_map/ppermute | solution.py:106
  225.9 26.6 %collective-permute-start.19 = (f32[6912]{0:T(1024)}, f32[6912]{0:T(1024)}, u32[]{:S(2)}, u32[]{:S(2)}) collective-permute-start(f32[6912]{0:T(1024)} %constant_dynamic-update-slice_fusion.4), channel_id=1, source_target_pairs={{0,1},{1,0},{2,3},{3,2},{4,5},{5,4},{6,7},{7,6},{8,9},{9,8},{10,11... | collective-permute-start | bytes 82952 | tf_op jit(solution)/shard_map/ppermute | solution.py:106
  229.5 37.9 %collective-permute-start.29 = (bf16[768,768]{1,0:T(8,128)(2,1)}, bf16[768,768]{1,0:T(8,128)(2,1)}, u32[]{:S(2)}, u32[]{:S(2)}) collective-permute-start(bf16[768,768]{1,0:T(8,128)(2,1)} %add_convert_fusion.3), channel_id=1, source_target_pairs={{0,2},{1,3},{2,0},{3,1},{4,6},{5,7},{6,4},{7,5},{8,10},{9,11},{10,... | collective-permute-start | bytes 3538952 | tf_op jit(solution)/shard_map/ppermute | solution.py:106
  245.2 163.8 %all-reduce.6.cloned.1.call-start = ((), (), s32[]{:S(2)}) async-start(), calls=%async_computation.1 | async-start | bytes 2359296 | tf_op jit(solution)/shard_map/psum | solution.py:232
  249.5 84.2 %collective-permute-start.24 = (bf16[768,768]{1,0:T(8,128)(2,1)}, bf16[768,768]{1,0:T(8,128)(2,1)}, u32[]{:S(2)}, u32[]{:S(2)}) collective-permute-start(bf16[768,768]{1,0:T(8,128)(2,1)} %select_convert_fusion.1), channel_id=1, source_target_pairs={{0,1},{1,0},{2,3},{3,2},{4,5},{5,4},{6,7},{7,6},{8,9},{9,8},{10,11... | collective-permute-start | bytes 3538952 | tf_op jit(solution)/shard_map/ppermute | solution.py:106
  252.0 81.7 %collective-permute-start.26 = (bf16[768,768]{1,0:T(8,128)(2,1)}, bf16[768,768]{1,0:T(8,128)(2,1)}, u32[]{:S(2)}, u32[]{:S(2)}) collective-permute-start(bf16[768,768]{1,0:T(8,128)(2,1)} %add_convert_fusion.5), channel_id=1, source_target_pairs={{0,2},{1,3},{2,0},{3,1},{4,6},{5,7},{6,4},{7,5},{8,10},{9,11},{10,... | collective-permute-start | bytes 3538952 | tf_op jit(solution)/shard_map/ppermute | solution.py:106
  325.7 166.8 %all-reduce.8.cloned.1.call-start = ((), (), s32[]{:S(2)}) async-start(), calls=%async_computation.2 | async-start | bytes 2359296 | tf_op jit(solution)/shard_map/psum | solution.py:267
  332.1 77.0 %collective-permute-start.21 = (f32[5760]{0:T(1024)S(1)}, f32[5760]{0:T(1024)S(1)}, u32[]{:S(2)}, u32[]{:S(2)}) collective-permute-start(f32[5760]{0:T(1024)S(1)} %pad_maximum_fusion.19), channel_id=1, source_target_pairs={{0,4},{4,0},{8,12},{12,8},{16,20},{20,16},{24,28},{28,24},{1,5},{5... | collective-permute-start | bytes 69128 | tf_op jit(solution)/shard_map/ppermute | solution.py:106
  (110 other events, 794.1 us)
Sparse Core Ops, SparseCore 0:
  245.3 80.3 all-reduce.3
  329.6 79.4 all-reduce.5
  413.1 79.3 all-reduce.7

commit v2 on v1

--- a/solution.py
+++ b/solution.py
@@ -122,15 +122,38 @@
     return [pieces[j] for j in range(count)]
 
 
-def reduce_pieces(pieces):
+def reduce_start(pieces):
     held = dict(enumerate(pieces))
-    for bit in bits_of(len(pieces)):
+    bits = bits_of(len(pieces))
+    for bit in bits[:-1]:
         held = {
             j: held[j] + swap(held[j ^ bit].astype(BF16), bit).astype(F32)
             for j in held
             if not j & bit
         }
-    return held[0]
+    return held[0], held[bits[-1]].astype(BF16)
+
+
+def reduce_finish(own, send, count):
+    return own + swap(send, bits_of(count)[-1]).astype(F32)
+
+
+def all_sum(values, bits):
+    me = lax.axis_index("dp")
+    for bit in bits:
+        upper = (me & bit) != 0
+        half = values.shape[0] // 2
+        low, high = values[:half], values[half:]
+        send = jnp.where(upper, low, high).astype(BF16)
+        values = jnp.where(upper, high, low) + swap(send, bit, "dp").astype(F32)
+    values = values.astype(BF16)
+    for bit in reversed(bits):
+        upper = (me & bit) != 0
+        got = swap(values, bit, "dp")
+        values = jnp.concatenate(
+            [jnp.where(upper, got, values), jnp.where(upper, values, got)], 0
+        )
+    return values
 
 
 def reorder(pieces, me, span):
@@ -174,9 +197,15 @@
     own_qkv = w_qkv.transpose(1, 2, 0).reshape(3 * local, width)
     own_bias = jnp.concatenate([b_qv.reshape(-1), b_fc])
     biases = gather_pieces(own_bias, count)
-    qkv = reorder(gather_pieces(own_qkv, count), me, span)
-    outs = reorder(gather_pieces(w_out, count), me, span)
+    qkv = gather_pieces(own_qkv, count)
+    far = bits_of(count)[-1]
+    qkv[far], w_out = lax.optimization_barrier((qkv[far], w_out))
+    qkv = reorder(qkv, me, span)
+    outs = gather_pieces(w_out, count)
+    outs[far], w_fc = lax.optimization_barrier((outs[far], w_fc))
+    outs = reorder(outs, me, span)
     fcs = gather_pieces(w_fc, count)
+    fcs[far], w_proj = lax.optimization_barrier((fcs[far], w_proj))
     projs = gather_pieces(w_proj, count)
     bqv = reorder([b[: 2 * local] for b in biases], me, span)
     bfc = [b[2 * local :] for b in biases]
@@ -227,9 +256,8 @@
         d_fc.append(mm(normed2, grad_pre, TN))
         grad_normed2 = grad_normed2 + mm(grad_pre, fcs[j], NT)
     output = result.astype(BF16)
-    g_proj = lax.psum(reduce_pieces(d_proj).astype(BF16), "dp")
-    own_fc, g_proj = lax.optimization_barrier((reduce_pieces(d_fc).astype(BF16), g_proj))
-    g_fc = lax.psum(own_fc, "dp")
+    own_proj, send_proj = reduce_start(d_proj)
+    own_fc, send_fc = reduce_start(d_fc)
 
     cot_full = cotangent.astype(F32)
     _, ln2_back = jax.vjp(layer_norm, residual, ln2_gain, ln2_bias)
@@ -239,6 +267,11 @@
     d_b_out = jnp.sum(grad_resid, 0)
     resid_low = grad_resid.astype(BF16)
     grad_mixed = mm(resid_low, wo, NT).astype(BF16)
+    grad_mixed, send_proj, send_fc = lax.optimization_barrier((grad_mixed, send_proj, send_fc))
+    bits = bits_of(lax.axis_size("dp"))
+    turned = bits[1:] + bits[:1]
+    own_proj = reduce_finish(own_proj, send_proj, count)
+    own_fc = reduce_finish(own_fc, send_fc, count)
     d_out = split_rows(mm(mixed, resid_low, TN), count)
     dq, dk, dv = attention_call(
         attend_back_kernel,
@@ -262,9 +295,10 @@
         jnp.concatenate([d_packed[0][c], d_packed[1][c], d_packed[2][c], d_out[c]], 0)
         for c in range(count)
     ]
-    own_attn = reduce_pieces(reorder(d_attn, me, span)).astype(BF16)
-    own_attn, g_fc = lax.optimization_barrier((own_attn, g_fc))
-    g_attn = lax.psum(own_attn, "dp")
+    own_attn = reduce_finish(*reduce_start(reorder(d_attn, me, span)), count)
+    g_proj = all_sum(own_proj, bits)
+    g_fc = all_sum(own_fc, turned)
+    g_attn = all_sum(own_attn, bits)
     d_bq = split_rows(jnp.sum(dq.astype(F32), 0), count)
     d_bv = split_rows(jnp.sum(dv.astype(F32), 0), count)
     d_bqv = reorder([jnp.concatenate([d_bq[c], d_bv[c]]) for c in range(count)], me, span)

time: 511 us -> 373 us (0.73)
  waiting for transfers between devices: 282 us -> 169 us
  starting transfers between devices: 17.8 us -> 47.4 us
  other arithmetic: 53.1 us -> 29.1 us
  between operations: 15.5 us -> 2.28 us
  local copies, waits for them, and re-layouts: 26.9 us -> 14.8 us
    psum x3 -> x0, waiting for transfers between devices: 196 us -> none  [the longest x1 71.7 us: on_device(): g_fc = lax.psum(own_fc, 'dp')]
    ppermute x33 -> x51, waiting for transfers between devices: 85.8 us -> 169 us  [swap(): return lax.ppermute(values, axis, [(i, i ^ bit) for i in range(size)])]
    ppermute x33 -> x51, starting transfers between devices: 17.6 us -> 47.4 us  [swap(): return lax.ppermute(values, axis, [(i, i ^ bit) for i in range(size)])]
    reduce_sum x2, other arithmetic: 14.3 us -> 1.94 us  [layer_norm(): center = values - jnp.mean(values, -1, keepdims=True)]
    convert_element_type x6 -> x15, other arithmetic: 17.4 us -> 6.39 us  [the longest x2 2.53 us: reduce_start(): held[j ^ bit].astype(BF16)]
    unnamed x197 -> x121, local copies, waits for them, and re-layouts: 11.9 us -> 3.64 us
    select_n x8, other arithmetic: 6.01 us -> 0.65 us  [reorder(): jnp.where(odd, pieces[c ^ bit], pieces[c])]
  transfers between devices with their start and end apart: 36 -> 51, of which waited for: 10 -> 23; matrix products, arithmetic and copies ran while one was open for 20% -> 26% of each run, Pallas kernels for 3% -> 12%
where the time goes in v2:
time: 373 us; the launch traced here: 366 us
  waiting for transfers between devices  169 us (45%)
  matrix products  59.7 us (16%)
  starting transfers between devices  47.4 us (13%)
  Pallas kernels  44.4 us (12%)
  other arithmetic  29.1 us (8%)
  local copies, waits for them, and re-layouts  14.8 us (4%)
    ppermute x51, waiting for transfers between devices, swap(): return lax.ppermute(values, axis, [(i, i ^ bit) for i in range(size)])  169 us
    dot_general x36, matrix products, mm(): return lax.dot_general(a, b, dims, preferred_element_type=F32)  59.7 us
    ppermute x51, starting transfers between devices, swap(): return lax.ppermute(values, axis, [(i, i ^ bit) for i in range(size)])  47.4 us
    pallas_call x2, Pallas kernels, attention_call(): pl.pallas_call(kernel, grid=(seqs, pairs), in_specs=[spec[kind] for kind...  44.4 us
    slice x6, local copies, waits for them, and re-layouts, split_rows(): return [values[c * step:(c + 1) * step] for c in range(count)]  7.69 us
  transfers between devices with their start and end apart: 51, of which 23 were waited for; matrix products, arithmetic and copies ran while one was open for 26% of the time, Pallas kernels for 12%

profile of v2, /device:TPU:0, one launch (start us, length us, event | category | flops | bytes accessed | tf_op | source)
XLA Modules:
  0.0 366.2 jit_solution(8796075893898834816)
XLA Ops:
  2.1 3.0 collective-permute-start.4
  11.6 15.8 %collective-permute-done.1 = bf16[576,768]{1,0:T(8,128)(2,1)S(1)} collective-permute-done((bf16[576,768]{1,0:T(8,128)(2,1)}, bf16[576,768]{1,0:T(8,128)(2,1)S(1)}, u32[]{:S(2)}, u32[]{:S(2)}) %collective-permute-start.1) | collective-permute-done | bytes 884768 | tf_op jit(solution)/shard_map/ppermute | solution.py:106
  28.5 8.5 %collective-permute-done.9 = bf16[192,768]{1,0:T(8,128)(2,1)S(1)} collective-permute-done((bf16[192,768]{1,0:T(8,128)(2,1)S(1)}, bf16[192,768]{1,0:T(8,128)(2,1)S(1)}, u32[]{:S(2)}, u32[]{:S(2)}) %collective-permute-start.9) | collective-permute-done | bytes 294944 | tf_op jit(solution)/shard_map/ppermute | solution.py:106
  42.8 21.9 %collective-permute-done.11 = bf16[768,768]{1,0:T(8,128)(2,1)} collective-permute-done((bf16[768,768]{1,0:T(8,128)(2,1)S(1)}, bf16[768,768]{1,0:T(8,128)(2,1)}, u32[]{:S(2)}, u32[]{:S(2)}) %collective-permute-start.11) | collective-permute-done | bytes 1179680 | tf_op jit(solution)/shard_map/ppermute | solution.py:106
  67.4 17.3 %shard_map.254 = (bf16[512,768]{1,0:T(8,128)(2,1)S(1)}, f32[512,768]{1,0:T(8,128)S(1)}) custom-call(bf16[512,768]{1,0:T(8,128)(2,1)S(1)} %add_convert_fusion.8.q_ref, bf16[1024,768]{1,0:T(8,128)(2,1)S(1)} %pad_maximum_fusion.4.k_ref, bf16[1024,768]{1,0:T(8,128)(2,1)} %pad_maximum_fusion.5.v_ref, f32[1,512,1024]{2,1,0:T(8,128)} %and_select_fusion.bias_ref), custom_call_target="tpu_custom_call" | custom-call | flops 6442450944 | bytes 6291456 | tf_op jit(solution)/shard_map/pallas_call | solution.py:88
  100.3 2.8 convert_reduce_fusion.4
  105.5 3.2 convert_reduce_fusion.2
  131.4 27.1 %shard_map.255 = (bf16[512,768]{1,0:T(8,128)(2,1)S(1)}, bf16[1024,768]{1,0:T(8,128)(2,1)S(1)}, bf16[1024,768]{1,0:T(8,128)(2,1)S(1)}) custom-call(bf16[512,768]{1,0:T(8,128)(2,1)S(1)} %add_convert_fusion.8.q_ref, bf16[1024,768]{1,0:T(8,128)(2,1)} %copy-done, bf16[1024,768]{1,0:T(8,128)(2,1)} %pad_maximum_fusion.5.v_ref, ...), custom_call_target="tpu_custom_call" | custom-call | flops 16106127360 | bytes 6291456 | tf_op jit(solution)/shard_map/pallas_call | solution.py:88
  170.4 3.9 %fusion.70 = f32[768,768]{1,0:T(8,128)} fusion(bf16[512,768]{1,0:T(8,128)(2,1)} %copy-done.43, bf16[1024,768]{1,0:T(8,128)(2,1)S(1)} %get-tuple-element.39, bf16[512,768]{1,0:T(8,128)(2,1)} %param.15, f32[768]{0:T(1024)S(1)} %copy-done.56, f32[768]{0:T(1024)S(1)} %copy-done.46, f32[512]{0:T(512)S(1)} %fusion.58, f32[512]{0:T(512)S(1)} %broadcast_multiply_fusion.1), kind=kOutput, calls=%fused_computation.233 | convolution fusion | flops 607911936 | bytes 4730880 | tf_op jit(solution)/shard_map/dot_general | solution.py:23
  178.4 2.8 fusion.89
  181.2 33.5 %collective-permute-done.22 = f32[5760]{0:T(1024)S(1)} collective-permute-done((f32[5760]{0:T(1024)S(1)}, f32[5760]{0:T(1024)S(1)}, u32[]{:S(2)}, u32[]{:S(2)}) %collective-permute-start.22) | collective-permute-done | bytes 23072 | tf_op jit(solution)/shard_map/ppermute | solution.py:106
  241.0 6.1 %collective-permute-done.37 = bf16[384,768]{1,0:T(8,128)(2,1)} collective-permute-done((bf16[384,768]{1,0:T(8,128)(2,1)}, bf16[384,768]{1,0:T(8,128)(2,1)}, u32[]{:S(2)}, u32[]{:S(2)}) %collective-permute-start.37) | collective-permute-done | bytes 589856 | tf_op jit(solution)/shard_map/ppermute | solution.py:106
  248.7 2.8 collective-permute-start.38
  258.8 5.5 %collective-permute-done.38 = bf16[192,768]{1,0:T(8,128)(2,1)S(1)} collective-permute-done((bf16[192,768]{1,0:T(8,128)(2,1)S(1)}, bf16[192,768]{1,0:T(8,128)(2,1)S(1)}, u32[]{:S(2)}, u32[]{:S(2)}) %collective-permute-start.38) | collective-permute-done | bytes 294944 | tf_op jit(solution)/shard_map/ppermute | solution.py:106
  272.1 12.0 %collective-permute-done.28 = bf16[768,768]{1,0:T(8,128)(2,1)S(1)} collective-permute-done((bf16[768,768]{1,0:T(8,128)(2,1)S(1)}, bf16[768,768]{1,0:T(8,128)(2,1)S(1)}, u32[]{:S(2)}, u32[]{:S(2)}) %collective-permute-start.28) | collective-permute-done | bytes 1179680 | tf_op jit(solution)/shard_map/ppermute | solution.py:106
  287.4 2.9 collective-permute-start.48
  290.5 8.6 %collective-permute-done.29 = bf16[384,768]{1,0:T(8,128)(2,1)S(1)} collective-permute-done((bf16[384,768]{1,0:T(8,128)(2,1)S(1)}, bf16[384,768]{1,0:T(8,128)(2,1)S(1)}, u32[]{:S(2)}, u32[]{:S(2)}) %collective-permute-start.29) | collective-permute-done | bytes 589856 | tf_op jit(solution)/shard_map/ppermute | solution.py:106
  303.0 11.4 %collective-permute-done.30 = bf16[192,768]{1,0:T(8,128)(2,1)S(1)} collective-permute-done((bf16[192,768]{1,0:T(8,128)(2,1)S(1)}, bf16[192,768]{1,0:T(8,128)(2,1)S(1)}, u32[]{:S(2)}, u32[]{:S(2)}) %collective-permute-start.30) | collective-permute-done | bytes 294944 | tf_op jit(solution)/shard_map/ppermute | solution.py:106
  318.1 5.4 %collective-permute-done.31 = bf16[96,768]{1,0:T(8,128)(2,1)S(1)} collective-permute-done((bf16[96,768]{1,0:T(8,128)(2,1)S(1)}, bf16[96,768]{1,0:T(8,128)(2,1)S(1)}, u32[]{:S(2)}, u32[]{:S(2)}) %collective-permute-start.31) | collective-permute-done | bytes 147488 | tf_op jit(solution)/shard_map/ppermute | solution.py:106
  323.9 9.9 %collective-permute-done.32 = bf16[96,768]{1,0:T(8,128)(2,1)S(1)} collective-permute-done((bf16[96,768]{1,0:T(8,128)(2,1)S(1)}, bf16[96,768]{1,0:T(8,128)(2,1)S(1)}, u32[]{:S(2)}, u32[]{:S(2)}) %collective-permute-start.32) | collective-permute-done | bytes 147488 | tf_op jit(solution)/shard_map/ppermute | solution.py:106
  333.9 3.0 collective-permute-start.33
  339.8 5.6 %collective-permute-done.33 = bf16[192,768]{1,0:T(8,128)(2,1)S(1)} collective-permute-done((bf16[192,768]{1,0:T(8,128)(2,1)S(1)}, bf16[192,768]{1,0:T(8,128)(2,1)S(1)}, u32[]{:S(2)}, u32[]{:S(2)}) %collective-permute-start.33) | collective-permute-done | bytes 294944 | tf_op jit(solution)/shard_map/ppermute | solution.py:106
  348.0 5.2 %collective-permute-done.50 = bf16[384,768]{1,0:T(8,128)(2,1)S(1)} collective-permute-done((bf16[384,768]{1,0:T(8,128)(2,1)S(1)}, bf16[384,768]{1,0:T(8,128)(2,1)S(1)}, u32[]{:S(2)}, u32[]{:S(2)}) %collective-permute-start.50) | collective-permute-done | bytes 589856 | tf_op jit(solution)/shard_map/ppermute | solution.py:106
  355.0 8.5 %collective-permute-done.34 = bf16[384,768]{1,0:T(8,128)(2,1)S(1)} collective-permute-done((bf16[384,768]{1,0:T(8,128)(2,1)S(1)}, bf16[384,768]{1,0:T(8,128)(2,1)S(1)}, u32[]{:S(2)}, u32[]{:S(2)}) %collective-permute-start.34) | collective-permute-done | bytes 589856 | tf_op jit(solution)/shard_map/ppermute | solution.py:106
  (360 shorter events, 137.3 us)
Async XLA Ops:
  5.1 22.3 %collective-permute-start.1 = (bf16[576,768]{1,0:T(8,128)(2,1)}, bf16[576,768]{1,0:T(8,128)(2,1)S(1)}, u32[]{:S(2)}, u32[]{:S(2)}) collective-permute-start(bf16[576,768]{1,0:T(8,128)(2,1)} %bitcast.108), channel_id=1, source_target_pairs={{0,2},{1,3},{2,0},{3,1},{4,6},{5,7},{6,4},{7,5},{8,10},{9,11},{10,... | collective-permute-start | bytes 2654216 | tf_op jit(solution)/shard_map/ppermute | solution.py:106
  5.2 23.0 %collective-permute-start = (bf16[576,768]{1,0:T(8,128)(2,1)}, bf16[576,768]{1,0:T(8,128)(2,1)S(1)}, u32[]{:S(2)}, u32[]{:S(2)}) collective-permute-start(bf16[576,768]{1,0:T(8,128)(2,1)} %bitcast.109), channel_id=1, source_target_pairs={{0,1},{1,0},{2,3},{3,2},{4,5},{5,4},{6,7},{7,6},{8,9},{9,8},{10,11... | collective-permute-start | bytes 2654216 | tf_op jit(solution)/shard_map/ppermute | solution.py:106
  37.0 27.7 %collective-permute-start.11 = (bf16[768,768]{1,0:T(8,128)(2,1)S(1)}, bf16[768,768]{1,0:T(8,128)(2,1)}, u32[]{:S(2)}, u32[]{:S(2)}) collective-permute-start(bf16[768,768]{1,0:T(8,128)(2,1)S(1)} %copy-done.51), channel_id=1, source_target_pairs={{0,2},{1,3},{2,0},{3,1},{4,6},{5,7},{6,4},{7,5},{8,10},{9,11},{10,... | collective-permute-start | bytes 3538952 | tf_op jit(solution)/shard_map/ppermute | solution.py:106
  37.4 50.3 %collective-permute-start.12 = (bf16[768,768]{1,0:T(8,128)(2,1)S(1)}, bf16[768,768]{1,0:T(8,128)(2,1)}, u32[]{:S(2)}, u32[]{:S(2)}) collective-permute-start(bf16[768,768]{1,0:T(8,128)(2,1)S(1)} %copy-done.51), channel_id=1, source_target_pairs={{0,1},{1,0},{2,3},{3,2},{4,5},{5,4},{6,7},{7,6},{8,9},{9,8},{10,11... | collective-permute-start | bytes 3538952 | tf_op jit(solution)/shard_map/ppermute | solution.py:106
  40.2 24.9 %collective-permute-start.6 = (bf16[512,768]{1,0:T(8,128)(2,1)S(1)}, bf16[512,768]{1,0:T(8,128)(2,1)S(1)}, u32[]{:S(2)}, u32[]{:S(2)}) collective-permute-start(bf16[512,768]{1,0:T(8,128)(2,1)S(1)} %convolution_convert_fusion.5), channel_id=1, source_target_pairs={{0,1},{1,0},{2,3},{3,2},{4,5},{5,4},{6,7},{7,6},{8,9},{9,8},{10,11... | collective-permute-start | bytes 2359304 | tf_op jit(solution)/shard_map/ppermute | solution.py:106
  41.2 24.5 %collective-permute-start.7 = (bf16[512,768]{1,0:T(8,128)(2,1)S(1)}, bf16[512,768]{1,0:T(8,128)(2,1)S(1)}, u32[]{:S(2)}, u32[]{:S(2)}) collective-permute-start(bf16[512,768]{1,0:T(8,128)(2,1)S(1)} %add_convert_fusion.7), channel_id=1, source_target_pairs={{0,1},{1,0},{2,3},{3,2},{4,5},{5,4},{6,7},{7,6},{8,9},{9,8},{10,11... | collective-permute-start | bytes 2359304 | tf_op jit(solution)/shard_map/ppermute | solution.py:106
  64.8 40.3 %collective-permute-start.14 = (bf16[768,768]{1,0:T(8,128)(2,1)S(1)}, bf16[768,768]{1,0:T(8,128)(2,1)}, u32[]{:S(2)}, u32[]{:S(2)}) collective-permute-start(bf16[768,768]{1,0:T(8,128)(2,1)S(1)} %copy-done.52), channel_id=1, source_target_pairs={{0,2},{1,3},{2,0},{3,1},{4,6},{5,7},{6,4},{7,5},{8,10},{9,11},{10,... | collective-permute-start | bytes 3538952 | tf_op jit(solution)/shard_map/ppermute | solution.py:106
  65.1 35.2 %collective-permute-start.13 = (bf16[768,768]{1,0:T(8,128)(2,1)S(1)}, bf16[768,768]{1,0:T(8,128)(2,1)}, u32[]{:S(2)}, u32[]{:S(2)}) collective-permute-start(bf16[768,768]{1,0:T(8,128)(2,1)S(1)} %copy-done.52), channel_id=1, source_target_pairs={{0,1},{1,0},{2,3},{3,2},{4,5},{5,4},{6,7},{7,6},{8,9},{9,8},{10,11... | collective-permute-start | bytes 3538952 | tf_op jit(solution)/shard_map/ppermute | solution.py:106
  65.1 32.8 %collective-permute-start.15 = (bf16[768,768]{1,0:T(8,128)(2,1)}, bf16[768,768]{1,0:T(8,128)(2,1)S(1)}, u32[]{:S(2)}, u32[]{:S(2)}) collective-permute-start(bf16[768,768]{1,0:T(8,128)(2,1)} %collective-permute-done.11), channel_id=1, source_target_pairs={{0,1},{1,0},{2,3},{3,2},{4,5},{5,4},{6,7},{7,6},{8,9},{9,8},{10,11... | collective-permute-start | bytes 3538952 | tf_op jit(solution)/shard_map/ppermute | solution.py:106
  92.3 141.0 %collective-permute-start.43 = (bf16[768,768]{1,0:T(8,128)(2,1)}, bf16[768,768]{1,0:T(8,128)(2,1)}, u32[]{:S(2)}, u32[]{:S(2)}) collective-permute-start(bf16[768,768]{1,0:T(8,128)(2,1)} %convolution_convert_fusion), channel_id=1, source_target_pairs={{0,1},{1,0},{2,3},{3,2},{4,5},{5,4},{6,7},{7,6},{8,9},{9,8},{10,11... | collective-permute-start | bytes 3538952 | tf_op jit(solution)/shard_map/ppermute | solution.py:106
  99.7 25.7 %collective-permute-start.17 = (bf16[768,768]{1,0:T(8,128)(2,1)S(1)}, bf16[768,768]{1,0:T(8,128)(2,1)S(1)}, u32[]{:S(2)}, u32[]{:S(2)}) collective-permute-start(bf16[768,768]{1,0:T(8,128)(2,1)S(1)} %convolution_convert_fusion.3), channel_id=1, source_target_pairs={{0,1},{1,0},{2,3},{3,2},{4,5},{5,4},{6,7},{7,6},{8,9},{9,8},{10,11... | collective-permute-start | bytes 3538952 | tf_op jit(solution)/shard_map/ppermute | solution.py:106
  105.0 122.4 %collective-permute-start.35 = (bf16[768,768]{1,0:T(8,128)(2,1)}, bf16[768,768]{1,0:T(8,128)(2,1)}, u32[]{:S(2)}, u32[]{:S(2)}) collective-permute-start(bf16[768,768]{1,0:T(8,128)(2,1)} %convolution_convert_fusion.1), channel_id=1, source_target_pairs={{0,1},{1,0},{2,3},{3,2},{4,5},{5,4},{6,7},{7,6},{8,9},{9,8},{10,11... | collective-permute-start | bytes 3538952 | tf_op jit(solution)/shard_map/ppermute | solution.py:106
  160.3 67.6 %collective-permute-start.36 = (bf16[768,768]{1,0:T(8,128)(2,1)}, bf16[768,768]{1,0:T(8,128)(2,1)}, u32[]{:S(2)}, u32[]{:S(2)}) collective-permute-start(bf16[768,768]{1,0:T(8,128)(2,1)} %add_convert_fusion.1), channel_id=1, source_target_pairs={{0,2},{1,3},{2,0},{3,1},{4,6},{5,7},{6,4},{7,5},{8,10},{9,11},{10,... | collective-permute-start | bytes 3538952 | tf_op jit(solution)/shard_map/ppermute | solution.py:106
  164.5 68.8 %collective-permute-start.44 = (bf16[768,768]{1,0:T(8,128)(2,1)}, bf16[768,768]{1,0:T(8,128)(2,1)}, u32[]{:S(2)}, u32[]{:S(2)}) collective-permute-start(bf16[768,768]{1,0:T(8,128)(2,1)} %add_convert_fusion.2), channel_id=1, source_target_pairs={{0,2},{1,3},{2,0},{3,1},{4,6},{5,7},{6,4},{7,5},{8,10},{9,11},{10,... | collective-permute-start | bytes 3538952 | tf_op jit(solution)/shard_map/ppermute | solution.py:106
  176.8 37.9 %collective-permute-start.22 = (f32[5760]{0:T(1024)S(1)}, f32[5760]{0:T(1024)S(1)}, u32[]{:S(2)}, u32[]{:S(2)}) collective-permute-start(f32[5760]{0:T(1024)S(1)} %pad_maximum_fusion.25), channel_id=1, source_target_pairs={{0,2},{1,3},{2,0},{3,1},{4,6},{5,7},{6,4},{7,5},{8,10},{9,11},{10,... | collective-permute-start | bytes 69128 | tf_op jit(solution)/shard_map/ppermute | solution.py:106
  227.4 28.3 %collective-permute-start.27 = (bf16[768,768]{1,0:T(8,128)(2,1)}, bf16[768,768]{1,0:T(8,128)(2,1)}, u32[]{:S(2)}, u32[]{:S(2)}) collective-permute-start(bf16[768,768]{1,0:T(8,128)(2,1)} %select_convert_fusion), channel_id=1, source_target_pairs={{0,1},{1,0},{2,3},{3,2},{4,5},{5,4},{6,7},{7,6},{8,9},{9,8},{10,11... | collective-permute-start | bytes 3538952 | tf_op jit(solution)/shard_map/ppermute | solution.py:106
  227.4 44.7 %collective-permute-start.26 = (bf16[768,768]{1,0:T(8,128)(2,1)}, bf16[768,768]{1,0:T(8,128)(2,1)}, u32[]{:S(2)}, u32[]{:S(2)}) collective-permute-start(bf16[768,768]{1,0:T(8,128)(2,1)} %select_convert_fusion.1), channel_id=1, source_target_pairs={{0,1},{1,0},{2,3},{3,2},{4,5},{5,4},{6,7},{7,6},{8,9},{9,8},{10,11... | collective-permute-start | bytes 3538952 | tf_op jit(solution)/shard_map/ppermute | solution.py:106
  257.2 26.9 %collective-permute-start.28 = (bf16[768,768]{1,0:T(8,128)(2,1)S(1)}, bf16[768,768]{1,0:T(8,128)(2,1)S(1)}, u32[]{:S(2)}, u32[]{:S(2)}) collective-permute-start(bf16[768,768]{1,0:T(8,128)(2,1)S(1)} %add_convert_fusion), channel_id=1, source_target_pairs={{0,2},{1,3},{2,0},{3,1},{4,6},{5,7},{6,4},{7,5},{8,10},{9,11},{10,... | collective-permute-start | bytes 3538952 | tf_op jit(solution)/shard_map/ppermute | solution.py:106
  268.0 19.4 %collective-permute-start.47 = (bf16[96,768]{1,0:T(8,128)(2,1)S(1)}, bf16[96,768]{1,0:T(8,128)(2,1)S(1)}, u32[]{:S(2)}, u32[]{:S(2)}) collective-permute-start(bf16[96,768]{1,0:T(8,128)(2,1)S(1)} %select_convert_fusion.8), channel_id=1, source_target_pairs={{0,16},{4,20},{8,24},{12,28},{16,0},{20,4},{24,8},{28,12},{1,17},{... | collective-permute-start | bytes 442376 | tf_op jit(solution)/shard_map/ppermute | solution.py:106
  270.5 19.8 %collective-permute-start.40 = (bf16[96,768]{1,0:T(8,128)(2,1)S(1)}, bf16[96,768]{1,0:T(8,128)(2,1)S(1)}, u32[]{:S(2)}, u32[]{:S(2)}) collective-permute-start(bf16[96,768]{1,0:T(8,128)(2,1)S(1)} %add_convert_fusion.10), channel_id=1, source_target_pairs={{0,4},{4,0},{8,12},{12,8},{16,20},{20,16},{24,28},{28,24},{1,5},{5... | collective-permute-start | bytes 442376 | tf_op jit(solution)/shard_map/ppermute | solution.py:106
  290.4 25.0 %collective-permute-start.41 = (bf16[192,768]{1,0:T(8,128)(2,1)S(1)}, bf16[192,768]{1,0:T(8,128)(2,1)S(1)}, u32[]{:S(2)}, u32[]{:S(2)}) collective-permute-start(bf16[192,768]{1,0:T(8,128)(2,1)S(1)} %pad_maximum_fusion.15), channel_id=1, source_target_pairs={{0,16},{4,20},{8,24},{12,28},{16,0},{20,4},{24,8},{28,12},{1,17},{... | collective-permute-start | bytes 884744 | tf_op jit(solution)/shard_map/ppermute | solution.py:106
  302.9 20.9 %collective-permute-start.49 = (bf16[192,768]{1,0:T(8,128)(2,1)S(1)}, bf16[192,768]{1,0:T(8,128)(2,1)S(1)}, u32[]{:S(2)}, u32[]{:S(2)}) collective-permute-start(bf16[192,768]{1,0:T(8,128)(2,1)S(1)} %pad_maximum_fusion.16), channel_id=1, source_target_pairs={{0,8},{4,12},{8,0},{12,4},{16,24},{20,28},{24,16},{28,20},{1,9},{5... | collective-permute-start | bytes 884744 | tf_op jit(solution)/shard_map/ppermute | solution.py:106
  315.5 24.1 %collective-permute-start.42 = (bf16[384,768]{1,0:T(8,128)(2,1)S(1)}, bf16[384,768]{1,0:T(8,128)(2,1)S(1)}, u32[]{:S(2)}, u32[]{:S(2)}) collective-permute-start(bf16[384,768]{1,0:T(8,128)(2,1)S(1)} %pad_maximum_fusion.12), channel_id=1, source_target_pairs={{0,8},{4,12},{8,0},{12,4},{16,24},{20,28},{24,16},{28,20},{1,9},{5... | collective-permute-start | bytes 1769480 | tf_op jit(solution)/shard_map/ppermute | solution.py:106
  345.5 18.0 %collective-permute-start.34 = (bf16[384,768]{1,0:T(8,128)(2,1)S(1)}, bf16[384,768]{1,0:T(8,128)(2,1)S(1)}, u32[]{:S(2)}, u32[]{:S(2)}) collective-permute-start(bf16[384,768]{1,0:T(8,128)(2,1)S(1)} %pad_maximum_fusion.11), channel_id=1, source_target_pairs={{0,4},{4,0},{8,12},{12,8},{16,20},{20,16},{24,28},{28,24},{1,5},{5... | collective-permute-start | bytes 1769480 | tf_op jit(solution)/shard_map/ppermute | solution.py:106
  (86 other events, 800.6 us)
